TPU v7x, 128 devices: a whole 4x4x4 slice. The times are simulated.
128 devices in a mesh: blk: 8 (over y_lo, x), grp: 16 (over y_hi, z, core).
Axes of the slice: x: 4, y: 4 (y_hi: 2, y_lo: 2; y = y_hi * 2 + y_lo), z: 4, core: 2. Of those that a mesh axis runs over, the one named last changes fastest.
Arguments:
- queries: bfloat16 [2048, 4096], P(('blk', 'grp')), may hold values from -2 to 2
- document_vectors: bfloat16 [2048, 4096], P(('blk', 'grp')), may hold values from -1.5 to 1.5
- negatives: bfloat16 [8192, 4096], P(('blk', 'grp')), may hold values from -1.5 to 1.5
- positives: int32 [2048], P(('blk', 'grp')), may hold values from 0 to 2047
- neg_ids: int32 [2048, 7], P(('blk', 'grp')), may hold values from 0 to 8191, as said below
Outputs:
- grad_queries: bfloat16 [2048, 4096], P(('blk', 'grp'))
- grad_passages: bfloat16 [2048, 4096], P(('blk', 'grp'))
- grad_negatives: bfloat16 [8192, 4096], P(('blk', 'grp'))
Inputs may be any that keep to these rules, and one draw needn't show every extreme that they name: `neg_ids`: row i holds the 7 negatives of query i as indices into negatives; the owner device of index n is n // 64. In the aligned blocks of 16 rows (the queries of one device) no owner device is named more than 2 times, and some owner exactly 2 times.
All inputs are finite; a program needn't handle non-finite values.
Results may differ from a plain program's by a relative error of at most 0.02.
Values may be sent and summed in bfloat16 or wider, within the bound.
A program may use at most 64 MiB of HBM per device.

v0:
```python
import jax
import jax.numpy as jnp
from jax import lax
from jax.sharding import PartitionSpec as P

sharpness_divisor = 0.02
floor_logit = -1e30


def passed_along(array, axis, by):
    peers = lax.axis_size(axis)
    return lax.ppermute(array, axis, [(i, (i + by) % peers) for i in range(peers)])


def merged(part, axis, combine):
    gathered = jax.tree.map(lambda a: lax.all_gather(a, axis), part)

    def take(source):
        return jax.tree.map(lambda a: lax.dynamic_index_in_dim(a, source, 0, False), gathered)

    return lax.fori_loop(
        1, lax.axis_size(axis), lambda source, state: combine(state, take(source)), take(0)
    )


def combine_stats(earlier, later):
    highest = jnp.maximum(earlier[0], later[0])
    summed = earlier[1] * jnp.exp(earlier[0] - highest) + later[1] * jnp.exp(later[0] - highest)
    return (highest, summed)


def rounded(values):
    return lax.optimization_barrier(values.astype(jnp.bfloat16)).astype(jnp.float32)


def on_device(queries, document_vectors, negatives, positives, neg_ids):
    blocks = lax.axis_size("blk")
    groups = lax.axis_size("grp")
    devices = blocks * groups
    rows_dev, feat_width = queries.shape
    hard_count = neg_ids.shape[1]
    pool_rows = negatives.shape[0]
    capacity = max(2, (3 * rows_dev * hard_count + 2 * devices - 1) // (2 * devices))
    here_blk = lax.axis_index("blk")
    here_grp = lax.axis_index("grp")
    entries = rows_dev * hard_count
    owner_dev = (neg_ids // pool_rows).reshape(entries)
    local_ids = (neg_ids % pool_rows).reshape(entries)
    onehot = (owner_dev[:, None] == jnp.arange(devices, dtype=jnp.int32)[None, :]).astype(jnp.int32)
    before = jnp.cumsum(onehot, 0) - onehot
    slot_index = jnp.sum(before * onehot, 1)
    position = owner_dev * capacity + slot_index
    request = (
        jnp.zeros((devices * capacity,), jnp.int32)
        .at[position]
        .set(local_ids)
        .reshape(devices, capacity)
    )
    asked_ids = lax.all_to_all(request, ("blk", "grp"), split_axis=0, concat_axis=0, tiled=True)
    asked_flat = asked_ids.reshape(devices * capacity)
    fetched = negatives[asked_flat].reshape(devices, capacity, feat_width)
    arrived = lax.all_to_all(fetched, ("blk", "grp"), split_axis=0, concat_axis=0, tiled=True)
    distractor_slab = arrived.reshape(devices * capacity, feat_width)[position].reshape(
        rows_dev, hard_count, feat_width
    )
    buffer = jnp.zeros((blocks, rows_dev, feat_width), jnp.bfloat16)
    buffer = lax.dynamic_update_index_in_dim(buffer, document_vectors, here_blk, 0)
    moving = document_vectors
    for stride in range(1, blocks):
        moving = passed_along(moving, "blk", 1)
        buffer = lax.dynamic_update_index_in_dim(buffer, moving, (here_blk - stride) % blocks, 0)
    candidate_passages = buffer.reshape(blocks * rows_dev, feat_width)
    gathered_q, gathered_pos = (
        lax.all_gather(queries, "grp", axis=0, tiled=True),
        lax.all_gather(positives, "grp", axis=0, tiled=True),
    )
    block_rows = rows_dev * groups
    affinity_matrix = (
        lax.dot_general(
            gathered_q,
            candidate_passages,
            (((1,), (1,)), ((), ())),
            preferred_element_type=jnp.float32,
        )
        / sharpness_divisor
    )
    mined_distractor_scaled_scores = (
        jnp.einsum("jy,jiy->ji", queries, distractor_slab, preferred_element_type=jnp.float32)
        / sharpness_divisor
    )
    column = (
        (jnp.arange(blocks, dtype=jnp.int32)[:, None] * groups + here_grp) * rows_dev
        + jnp.arange(rows_dev, dtype=jnp.int32)[None, :]
    ).reshape(blocks * rows_dev)
    local_top = jnp.max(affinity_matrix, 1)
    local_sum = jnp.sum(jnp.exp(affinity_matrix - local_top[:, None]), 1)
    hard_top = jnp.max(mined_distractor_scaled_scores, 1)
    hard_sum = jnp.sum(jnp.exp(mined_distractor_scaled_scores - hard_top[:, None]), 1)
    offset = here_grp * rows_dev
    hard_top_all = lax.dynamic_update_slice_in_dim(
        jnp.full((block_rows,), floor_logit, jnp.float32), hard_top, offset, 0
    )
    hard_sum_all = lax.dynamic_update_slice_in_dim(
        jnp.zeros((block_rows,), jnp.float32), hard_sum, offset, 0
    )
    joined = combine_stats((local_top, local_sum), (hard_top_all, hard_sum_all))
    highest, summed = merged(joined, "grp", combine_stats)
    log_total = highest + jnp.log(summed)
    target = (column[None, :] == gathered_pos[:, None]).astype(jnp.float32)
    normalized_likelihoods = (jnp.exp(affinity_matrix - log_total[:, None]) - target).astype(
        jnp.bfloat16
    )
    home_log = lax.dynamic_slice_in_dim(log_total, offset, rows_dev, 0)
    mined_distractor_likelihoods = jnp.exp(
        mined_distractor_scaled_scores - home_log[:, None]
    ).astype(jnp.bfloat16)
    selected_rows = normalized_likelihoods
    batch_part = lax.psum_scatter(
        (
            jnp.dot(selected_rows, candidate_passages, preferred_element_type=jnp.float32)
            / sharpness_divisor
        ).astype(jnp.bfloat16),
        "grp",
        scatter_dimension=0,
        tiled=True,
    ).astype(jnp.float32)
    mined_distractor_share = (
        jnp.einsum(
            "he,her->hr",
            mined_distractor_likelihoods,
            distractor_slab,
            preferred_element_type=jnp.float32,
        )
        / sharpness_divisor
    )
    grad_queries = (batch_part + mined_distractor_share).astype(jnp.bfloat16)

    def passage_term(first_row, row_count):
        selected_rows = lax.dynamic_slice_in_dim(normalized_likelihoods, first_row, row_count, 1)
        return (
            lax.dot_general(
                selected_rows,
                gathered_q,
                (((0,), (0,)), ((), ())),
                preferred_element_type=jnp.float32,
            )
            / sharpness_divisor
        )

    carried = rounded(passage_term(here_blk * rows_dev, rows_dev))
    for stride in range(blocks):
        carried = passed_along(carried.astype(jnp.bfloat16), "blk", 1).astype(carried.dtype)
        if stride < blocks - 1:
            carried = carried + rounded(
                passage_term((here_blk - stride - 1) % blocks * rows_dev, rows_dev)
            )
    grad_passages = carried.astype(jnp.bfloat16)
    mined_distractor_grads = (
        mined_distractor_likelihoods.astype(jnp.float32)[:, :, None]
        * queries.astype(jnp.float32)[:, None, :]
        / sharpness_divisor
    )
    mined_distractor_grads = mined_distractor_grads.astype(jnp.bfloat16).reshape(
        entries, feat_width
    )
    outgoing = (
        jnp.zeros((devices * capacity, feat_width), jnp.bfloat16)
        .at[position]
        .set(mined_distractor_grads)
    )
    outgoing = outgoing.reshape(devices, capacity, feat_width)
    returned = lax.all_to_all(outgoing, ("blk", "grp"), split_axis=0, concat_axis=0, tiled=True)
    returned = returned.reshape(devices * capacity, feat_width)
    matches = (asked_flat[:, None] == jnp.arange(pool_rows, dtype=jnp.int32)[None, :]).astype(
        jnp.bfloat16
    )
    grad_negatives = lax.dot_general(
        matches, returned, (((0,), (0,)), ((), ())), preferred_element_type=jnp.float32
    ).astype(jnp.bfloat16)
    return (grad_queries, grad_passages, grad_negatives)


def solution(mesh):
    placed = (
        P(("blk", "grp"), None),
        P(("blk", "grp"), None),
        P(("blk", "grp"), None),
        P(("blk", "grp")),
        P(("blk", "grp"), None),
    )
    return jax.shard_map(
        on_device,
        mesh=mesh,
        in_specs=placed,
        out_specs=(P(("blk", "grp"), None), P(("blk", "grp"), None), P(("blk", "grp"), None)),
        check_vma=False,
    )
```

profile of v0, /device:TPU:0, one launch (start us, length us, event | category | flops | bytes accessed | tf_op | source)
XLA Modules:
  0.0 282.8 jit_solution(6925222013987251267)
XLA Ops:
  10.6 11.1 %all-to-all-start = ((s32[128,1,2]{2,1,0:T(1,128)}), s32[128,1,2]{2,1,0:T(1,128)S(1)}, u32[]{:S(2)}, u32[]{:S(2)}) async-start(s32[128,1,2]{2,1,0:T(1,128)} %bitcast.13), calls=%async_computation | async-start | bytes 131072 | tf_op jit(solution)/shard_map/all_to_all | solution.py:59
  27.7 14.5 %all-reduce = s32[256]{0:T(256)S(1)} all-reduce(s32[256]{0:T(256)S(1)} %dynamic-update-slice), channel_id=1, replica_groups=mesh['blk'=8,'grp'=16] {'grp'}, use_global_device_ids=true, to_apply=%add | all-reduce | flops 256 | bytes 2048
  43.7 3.2 %gather_fusion = bf16[256,4096]{1,0:T(8,128)(2,1)} fusion(bf16[64,4096]{1,0:T(8,128)(2,1)S(1)} %copy-done, s32[1024]{0:T(1024)S(1)} %pad_clamp_fusion.1), kind=kCustom, calls=%fused_computation | custom fusion | bytes 4195328 | tf_op jit(solution)/shard_map/gather | solution.py:61
  46.8 4.4 %reshape.133 = bf16[128,2,4096]{2,1,0:T(2,128)(2,1)} reshape(bf16[256,4096]{1,0:T(8,128)(2,1)} %gather_fusion) | data formatting | bytes 4194304 | tf_op jit(solution)/shard_map/reshape | solution.py:61
  51.2 5.8 %all-to-all-start.1 = ((bf16[128,2,4096]{2,1,0:T(2,128)(2,1)}), bf16[128,2,4096]{2,1,0:T(2,128)(2,1)}, u32[]{:S(2)}, u32[]{:S(2)}) async-start(bf16[128,2,4096]{2,1,0:T(2,128)(2,1)} %reshape.133), calls=%async_computation.1 | async-start | bytes 4194304 | tf_op jit(solution)/shard_map/all_to_all | solution.py:62
  58.1 27.0 %collective-permute-done.1 = bf16[16,4096]{1,0:T(8,128)(2,1)S(1)} collective-permute-done((bf16[16,4096]{1,0:T(8,128)(2,1)S(1)}, bf16[16,4096]{1,0:T(8,128)(2,1)S(1)}, u32[]{:S(2)}, u32[]{:S(2)}) %collective-permute-start.1) | collective-permute-done | bytes 131104 | tf_op jit(solution)/shard_map/ppermute | solution.py:12
  85.2 7.2 %collective-permute-done.2 = bf16[16,4096]{1,0:T(8,128)(2,1)S(1)} collective-permute-done((bf16[16,4096]{1,0:T(8,128)(2,1)S(1)}, bf16[16,4096]{1,0:T(8,128)(2,1)S(1)}, u32[]{:S(2)}, u32[]{:S(2)}) %collective-permute-start.2) | collective-permute-done | bytes 131104 | tf_op jit(solution)/shard_map/ppermute | solution.py:12
  92.4 7.1 %collective-permute-done.3 = bf16[16,4096]{1,0:T(8,128)(2,1)S(1)} collective-permute-done((bf16[16,4096]{1,0:T(8,128)(2,1)S(1)}, bf16[16,4096]{1,0:T(8,128)(2,1)S(1)}, u32[]{:S(2)}, u32[]{:S(2)}) %collective-permute-start.3) | collective-permute-done | bytes 131104 | tf_op jit(solution)/shard_map/ppermute | solution.py:12
  99.5 7.1 %collective-permute-done.4 = bf16[16,4096]{1,0:T(8,128)(2,1)S(1)} collective-permute-done((bf16[16,4096]{1,0:T(8,128)(2,1)S(1)}, bf16[16,4096]{1,0:T(8,128)(2,1)S(1)}, u32[]{:S(2)}, u32[]{:S(2)}) %collective-permute-start.4) | collective-permute-done | bytes 131104 | tf_op jit(solution)/shard_map/ppermute | solution.py:12
  106.6 7.1 %collective-permute-done.5 = bf16[16,4096]{1,0:T(8,128)(2,1)S(1)} collective-permute-done((bf16[16,4096]{1,0:T(8,128)(2,1)S(1)}, bf16[16,4096]{1,0:T(8,128)(2,1)S(1)}, u32[]{:S(2)}, u32[]{:S(2)}) %collective-permute-start.5) | collective-permute-done | bytes 131104 | tf_op jit(solution)/shard_map/ppermute | solution.py:12
  113.7 7.1 %collective-permute-done.6 = bf16[16,4096]{1,0:T(8,128)(2,1)S(1)} collective-permute-done((bf16[16,4096]{1,0:T(8,128)(2,1)S(1)}, bf16[16,4096]{1,0:T(8,128)(2,1)S(1)}, u32[]{:S(2)}, u32[]{:S(2)}) %collective-permute-start.6) | collective-permute-done | bytes 131104 | tf_op jit(solution)/shard_map/ppermute | solution.py:12
  131.1 24.8 %all-gather.2 = f32[16,1,256]{2,1,0:T(1,128)S(1)} all-gather(f32[1,1,256]{2,1,0:T(1,128)S(1)} %bitcast.88), channel_id=2, replica_groups=mesh['blk'=8,'grp'=16] {'grp'}, dimensions={0}, use_global_device_ids=true | all-gather | bytes 17408 | tf_op jit(solution)/shard_map/all_gather | solution.py:16
  155.9 19.4 %all-gather.3 = f32[16,1,256]{2,1,0:T(1,128)S(1)} all-gather(f32[1,1,256]{2,1,0:T(1,128)S(1)} %bitcast.87), channel_id=3, replica_groups=mesh['blk'=8,'grp'=16] {'grp'}, dimensions={0}, use_global_device_ids=true | all-gather | bytes 17408 | tf_op jit(solution)/shard_map/all_gather | solution.py:16
  176.4 3.4 %fusion = bf16[256,4096]{1,0:T(8,128)(2,1)} fusion(bf16[256,128]{0,1:T(8,128)(2,1)S(1)} %fusion.17, bf16[128,4096]{1,0:T(8,128)(2,1)} %bitcast.73), kind=kOutput, calls=%fused_computation.8 | convolution fusion | flops 270532608 | bytes 3211264 | tf_op jit(solution)/shard_map/dot_general | solution.py:120
  181.1 7.0 %collective-permute-done.7 = bf16[16,4096]{1,0:T(8,128)(2,1)S(1)} collective-permute-done((bf16[16,4096]{1,0:T(8,128)(2,1)S(1)}, bf16[16,4096]{1,0:T(8,128)(2,1)S(1)}, u32[]{:S(2)}, u32[]{:S(2)}) %collective-permute-start.7) | collective-permute-done | bytes 131104 | tf_op jit(solution)/shard_map/ppermute | solution.py:12
  188.6 6.7 %collective-permute-done.8 = bf16[16,4096]{1,0:T(8,128)(2,1)S(1)} collective-permute-done((bf16[16,4096]{1,0:T(8,128)(2,1)S(1)}, bf16[16,4096]{1,0:T(8,128)(2,1)S(1)}, u32[]{:S(2)}, u32[]{:S(2)}) %collective-permute-start.8) | collective-permute-done | bytes 131104 | tf_op jit(solution)/shard_map/ppermute | solution.py:12
  195.8 6.7 %collective-permute-done.9 = bf16[16,4096]{1,0:T(8,128)(2,1)S(1)} collective-permute-done((bf16[16,4096]{1,0:T(8,128)(2,1)S(1)}, bf16[16,4096]{1,0:T(8,128)(2,1)S(1)}, u32[]{:S(2)}, u32[]{:S(2)}) %collective-permute-start.9) | collective-permute-done | bytes 131104 | tf_op jit(solution)/shard_map/ppermute | solution.py:12
  203.0 6.7 %collective-permute-done.10 = bf16[16,4096]{1,0:T(8,128)(2,1)S(1)} collective-permute-done((bf16[16,4096]{1,0:T(8,128)(2,1)S(1)}, bf16[16,4096]{1,0:T(8,128)(2,1)S(1)}, u32[]{:S(2)}, u32[]{:S(2)}) %collective-permute-start.10) | collective-permute-done | bytes 131104 | tf_op jit(solution)/shard_map/ppermute | solution.py:12
  210.2 6.8 %collective-permute-done.11 = bf16[16,4096]{1,0:T(8,128)(2,1)S(1)} collective-permute-done((bf16[16,4096]{1,0:T(8,128)(2,1)S(1)}, bf16[16,4096]{1,0:T(8,128)(2,1)S(1)}, u32[]{:S(2)}, u32[]{:S(2)}) %collective-permute-start.11) | collective-permute-done | bytes 131104 | tf_op jit(solution)/shard_map/ppermute | solution.py:12
  217.2 4.5 %scatter_custom_fusion.1 = bf16[256,4096]{1,0:T(8,128)(2,1)} fusion(s32[112]{0:T(128)} %copy-done.7, bf16[]{:T(256)} %constant.214.clone.1, f32[112,4096]{1,0:T(8,128)} %mul.129, f32[]{:T(128)} %constant.227.clone.1, f32[112]{0:T(128)S(1)} %reshape.138), kind=kCustom, calls=%fused_computation.28 | custom fusion | flops 1376256 | bytes 3933632 | tf_op jit(solution)/shard_map/scatter | solution.py:169
  221.8 4.4 %reshape.136 = bf16[128,2,4096]{2,1,0:T(2,128)(2,1)} reshape(bf16[256,4096]{1,0:T(8,128)(2,1)} %scatter_custom_fusion.1) | data formatting | bytes 4194304 | tf_op jit(solution)/shard_map/reshape | solution.py:171
  226.1 7.7 %all-to-all-start.2 = ((bf16[128,2,4096]{2,1,0:T(2,128)(2,1)}), bf16[128,2,4096]{2,1,0:T(2,128)(2,1)}, u32[]{:S(2)}, u32[]{:S(2)}) async-start(bf16[128,2,4096]{2,1,0:T(2,128)(2,1)} %reshape.136), calls=%async_computation.3 | async-start | bytes 4194304 | tf_op jit(solution)/shard_map/all_to_all | solution.py:172
  235.3 26.8 %collective-permute-done.13 = bf16[16,4096]{1,0:T(8,128)(2,1)S(1)} collective-permute-done((bf16[16,4096]{1,0:T(8,128)(2,1)S(1)}, bf16[16,4096]{1,0:T(8,128)(2,1)S(1)}, u32[]{:S(2)}, u32[]{:S(2)}) %collective-permute-start.13) | collective-permute-done | bytes 131104 | tf_op jit(solution)/shard_map/ppermute | solution.py:12
  262.6 6.8 %collective-permute-done.14 = bf16[16,4096]{1,0:T(8,128)(2,1)S(1)} collective-permute-done((bf16[16,4096]{1,0:T(8,128)(2,1)S(1)}, bf16[16,4096]{1,0:T(8,128)(2,1)S(1)}, u32[]{:S(2)}, u32[]{:S(2)}) %collective-permute-start.14) | collective-permute-done | bytes 131104 | tf_op jit(solution)/shard_map/ppermute | solution.py:12
  (156 shorter events, 34.5 us)
Async XLA Ops:
  7.2 36.5 %copy-start = (bf16[64,4096]{1,0:T(8,128)(2,1)S(1)}, bf16[64,4096]{1,0:T(8,128)(2,1)}, u32[]{:S(2)}) copy-start(bf16[64,4096]{1,0:T(8,128)(2,1)} %param.9) | copy-start | bytes 1572868
  8.9 14.3 %copy-start.7 = (s32[112]{0:T(128)}, s32[112]{0:T(128)S(1)}, u32[]{:S(2)}) copy-start(s32[112]{0:T(128)S(1)} %fusion.40) | copy-start | bytes 1348
  10.6 31.5 %all-to-all-start = ((s32[128,1,2]{2,1,0:T(1,128)}), s32[128,1,2]{2,1,0:T(1,128)S(1)}, u32[]{:S(2)}, u32[]{:S(2)}) async-start(s32[128,1,2]{2,1,0:T(1,128)} %bitcast.13), calls=%async_computation | async-start | bytes 131072 | tf_op jit(solution)/shard_map/all_to_all | solution.py:59
  21.8 106.8 %all-gather.6.cloned.1.call-start = ((), (), s32[]{:S(2)}) async-start(), calls=%async_computation.4 | async-start | bytes 2228224 | tf_op jit(solution)/shard_map/all_gather | solution.py:74
  21.8 35.4 %collective-permute-start = (bf16[16,4096]{1,0:T(8,128)(2,1)}, bf16[16,4096]{1,0:T(8,128)(2,1)S(1)}, u32[]{:S(2)}, u32[]{:S(2)}) collective-permute-start(bf16[16,4096]{1,0:T(8,128)(2,1)} %param.8), channel_id=1, source_target_pairs={{0,16},{16,32},{32,48},{48,64},{64,80},{80,96},{96,112},{112,0},{1... | collective-permute-start | bytes 393224 | tf_op jit(solution)/shard_map/ppermute | solution.py:12
  51.2 70.5 %all-to-all-start.1 = ((bf16[128,2,4096]{2,1,0:T(2,128)(2,1)}), bf16[128,2,4096]{2,1,0:T(2,128)(2,1)}, u32[]{:S(2)}, u32[]{:S(2)}) async-start(bf16[128,2,4096]{2,1,0:T(2,128)(2,1)} %reshape.133), calls=%async_computation.1 | async-start | bytes 4194304 | tf_op jit(solution)/shard_map/all_to_all | solution.py:62
  57.0 216.5 %reduce-scatter.2.cloned.1.call-start = ((), (), s32[]{:S(2)}) async-start(), calls=%async_computation.5 | async-start | bytes 2228224 | tf_op jit(solution)/shard_map/reduce_scatter | solution.py:118
  57.2 27.9 %collective-permute-start.1 = (bf16[16,4096]{1,0:T(8,128)(2,1)S(1)}, bf16[16,4096]{1,0:T(8,128)(2,1)S(1)}, u32[]{:S(2)}, u32[]{:S(2)}) collective-permute-start(bf16[16,4096]{1,0:T(8,128)(2,1)S(1)} %collective-permute-done), channel_id=1, source_target_pairs={{0,16},{16,32},{32,48},{48,64},{64,80},{80,96},{96,112},{112,0},{1... | collective-permute-start | bytes 393224 | tf_op jit(solution)/shard_map/ppermute | solution.py:12
  85.1 7.3 %collective-permute-start.2 = (bf16[16,4096]{1,0:T(8,128)(2,1)S(1)}, bf16[16,4096]{1,0:T(8,128)(2,1)S(1)}, u32[]{:S(2)}, u32[]{:S(2)}) collective-permute-start(bf16[16,4096]{1,0:T(8,128)(2,1)S(1)} %collective-permute-done.1), channel_id=1, source_target_pairs={{0,16},{16,32},{32,48},{48,64},{64,80},{80,96},{96,112},{112,0},{1... | collective-permute-start | bytes 393224 | tf_op jit(solution)/shard_map/ppermute | solution.py:12
  92.4 7.1 %collective-permute-start.3 = (bf16[16,4096]{1,0:T(8,128)(2,1)S(1)}, bf16[16,4096]{1,0:T(8,128)(2,1)S(1)}, u32[]{:S(2)}, u32[]{:S(2)}) collective-permute-start(bf16[16,4096]{1,0:T(8,128)(2,1)S(1)} %collective-permute-done.2), channel_id=1, source_target_pairs={{0,16},{16,32},{32,48},{48,64},{64,80},{80,96},{96,112},{112,0},{1... | collective-permute-start | bytes 393224 | tf_op jit(solution)/shard_map/ppermute | solution.py:12
  99.5 7.1 %collective-permute-start.4 = (bf16[16,4096]{1,0:T(8,128)(2,1)S(1)}, bf16[16,4096]{1,0:T(8,128)(2,1)S(1)}, u32[]{:S(2)}, u32[]{:S(2)}) collective-permute-start(bf16[16,4096]{1,0:T(8,128)(2,1)S(1)} %collective-permute-done.3), channel_id=1, source_target_pairs={{0,16},{16,32},{32,48},{48,64},{64,80},{80,96},{96,112},{112,0},{1... | collective-permute-start | bytes 393224 | tf_op jit(solution)/shard_map/ppermute | solution.py:12
  106.6 7.1 %collective-permute-start.5 = (bf16[16,4096]{1,0:T(8,128)(2,1)S(1)}, bf16[16,4096]{1,0:T(8,128)(2,1)S(1)}, u32[]{:S(2)}, u32[]{:S(2)}) collective-permute-start(bf16[16,4096]{1,0:T(8,128)(2,1)S(1)} %collective-permute-done.4), channel_id=1, source_target_pairs={{0,16},{16,32},{32,48},{48,64},{64,80},{80,96},{96,112},{112,0},{1... | collective-permute-start | bytes 393224 | tf_op jit(solution)/shard_map/ppermute | solution.py:12
  113.6 7.1 %collective-permute-start.6 = (bf16[16,4096]{1,0:T(8,128)(2,1)S(1)}, bf16[16,4096]{1,0:T(8,128)(2,1)S(1)}, u32[]{:S(2)}, u32[]{:S(2)}) collective-permute-start(bf16[16,4096]{1,0:T(8,128)(2,1)S(1)} %collective-permute-done.5), channel_id=1, source_target_pairs={{0,16},{16,32},{32,48},{48,64},{64,80},{80,96},{96,112},{112,0},{1... | collective-permute-start | bytes 393224 | tf_op jit(solution)/shard_map/ppermute | solution.py:12
  125.9 5.1 %copy-start.4 = (bf16[16,7,4096]{2,1,0:T(8,128)(2,1)}, bf16[16,7,4096]{2,1,0:T(8,128)(2,1)S(1)}, u32[]{:S(2)}) copy-start(bf16[16,7,4096]{2,1,0:T(8,128)(2,1)S(1)} %reshape.135) | copy-start | bytes 2752516
  180.2 7.9 %collective-permute-start.7 = (bf16[16,4096]{1,0:T(8,128)(2,1)S(1)}, bf16[16,4096]{1,0:T(8,128)(2,1)S(1)}, u32[]{:S(2)}, u32[]{:S(2)}) collective-permute-start(bf16[16,4096]{1,0:T(8,128)(2,1)S(1)} %fusion.1), channel_id=1, source_target_pairs={{0,16},{16,32},{32,48},{48,64},{64,80},{80,96},{96,112},{112,0},{1... | collective-permute-start | bytes 393224 | tf_op jit(solution)/shard_map/ppermute | solution.py:12
  188.1 7.1 %collective-permute-start.8 = (bf16[16,4096]{1,0:T(8,128)(2,1)S(1)}, bf16[16,4096]{1,0:T(8,128)(2,1)S(1)}, u32[]{:S(2)}, u32[]{:S(2)}) collective-permute-start(bf16[16,4096]{1,0:T(8,128)(2,1)S(1)} %add_convert_fusion.6), channel_id=1, source_target_pairs={{0,16},{16,32},{32,48},{48,64},{64,80},{80,96},{96,112},{112,0},{1... | collective-permute-start | bytes 393224 | tf_op jit(solution)/shard_map/ppermute | solution.py:12
  195.3 7.1 %collective-permute-start.9 = (bf16[16,4096]{1,0:T(8,128)(2,1)S(1)}, bf16[16,4096]{1,0:T(8,128)(2,1)S(1)}, u32[]{:S(2)}, u32[]{:S(2)}) collective-permute-start(bf16[16,4096]{1,0:T(8,128)(2,1)S(1)} %add_convert_fusion.5), channel_id=1, source_target_pairs={{0,16},{16,32},{32,48},{48,64},{64,80},{80,96},{96,112},{112,0},{1... | collective-permute-start | bytes 393224 | tf_op jit(solution)/shard_map/ppermute | solution.py:12
  202.5 7.1 %collective-permute-start.10 = (bf16[16,4096]{1,0:T(8,128)(2,1)S(1)}, bf16[16,4096]{1,0:T(8,128)(2,1)S(1)}, u32[]{:S(2)}, u32[]{:S(2)}) collective-permute-start(bf16[16,4096]{1,0:T(8,128)(2,1)S(1)} %add_convert_fusion.4), channel_id=1, source_target_pairs={{0,16},{16,32},{32,48},{48,64},{64,80},{80,96},{96,112},{112,0},{1... | collective-permute-start | bytes 393224 | tf_op jit(solution)/shard_map/ppermute | solution.py:12
  209.7 7.2 %collective-permute-start.11 = (bf16[16,4096]{1,0:T(8,128)(2,1)S(1)}, bf16[16,4096]{1,0:T(8,128)(2,1)S(1)}, u32[]{:S(2)}, u32[]{:S(2)}) collective-permute-start(bf16[16,4096]{1,0:T(8,128)(2,1)S(1)} %add_convert_fusion.3), channel_id=1, source_target_pairs={{0,16},{16,32},{32,48},{48,64},{64,80},{80,96},{96,112},{112,0},{1... | collective-permute-start | bytes 393224 | tf_op jit(solution)/shard_map/ppermute | solution.py:12
  217.0 16.9 %collective-permute-start.12 = (bf16[16,4096]{1,0:T(8,128)(2,1)S(1)}, bf16[16,4096]{1,0:T(8,128)(2,1)S(1)}, u32[]{:S(2)}, u32[]{:S(2)}) collective-permute-start(bf16[16,4096]{1,0:T(8,128)(2,1)S(1)} %add_convert_fusion.2), channel_id=1, source_target_pairs={{0,16},{16,32},{32,48},{48,64},{64,80},{80,96},{96,112},{112,0},{1... | collective-permute-start | bytes 393224 | tf_op jit(solution)/shard_map/ppermute | solution.py:12
  226.1 43.3 %all-to-all-start.2 = ((bf16[128,2,4096]{2,1,0:T(2,128)(2,1)}), bf16[128,2,4096]{2,1,0:T(2,128)(2,1)}, u32[]{:S(2)}, u32[]{:S(2)}) async-start(bf16[128,2,4096]{2,1,0:T(2,128)(2,1)} %reshape.136), calls=%async_computation.3 | async-start | bytes 4194304 | tf_op jit(solution)/shard_map/all_to_all | solution.py:172
  233.9 28.3 %copy-start.5 = (bf16[16,7,4096]{2,1,0:T(8,128)(2,1)S(1)}, bf16[16,7,4096]{2,1,0:T(8,128)(2,1)}, u32[]{:S(2)}) copy-start(bf16[16,7,4096]{2,1,0:T(8,128)(2,1)} %copy-done.4) | copy-start | bytes 2752516
  234.0 28.1 %collective-permute-start.13 = (bf16[16,4096]{1,0:T(8,128)(2,1)S(1)}, bf16[16,4096]{1,0:T(8,128)(2,1)S(1)}, u32[]{:S(2)}, u32[]{:S(2)}) collective-permute-start(bf16[16,4096]{1,0:T(8,128)(2,1)S(1)} %add_convert_fusion.1), channel_id=1, source_target_pairs={{0,16},{16,32},{32,48},{48,64},{64,80},{80,96},{96,112},{112,0},{1... | collective-permute-start | bytes 393224 | tf_op jit(solution)/shard_map/ppermute | solution.py:12
  262.1 7.3 %collective-permute-start.14 = (bf16[16,4096]{1,0:T(8,128)(2,1)S(1)}, bf16[16,4096]{1,0:T(8,128)(2,1)S(1)}, u32[]{:S(2)}, u32[]{:S(2)}) collective-permute-start(bf16[16,4096]{1,0:T(8,128)(2,1)S(1)} %add_convert_fusion), channel_id=1, source_target_pairs={{0,16},{16,32},{32,48},{48,64},{64,80},{80,96},{96,112},{112,0},{1... | collective-permute-start | bytes 393224 | tf_op jit(solution)/shard_map/ppermute | solution.py:12
  (6 other events, 13.8 us)
Sparse Core Ops, SparseCore 0:
  25.1 72.9 all-gather.5
  179.9 84.2 reduce-scatter.1
where the time goes:
time: 283 us
  waiting for transfers between devices  130 us (46%)
  blocking collectives  58.8 us (21%)
  local copies, waits for them, and re-layouts  28.1 us (10%)
  starting transfers between devices  28.1 us (10%)
  between operations  15.5 us (5%)
  matrix products  12.6 us (4%)
  other arithmetic  9.41 us (3%)
    ppermute x15, waiting for transfers between devices, passed_along(): lax.ppermute(array, axis, [(i, (i + by) % peers) for i in range(peers)])  130 us
    all_gather x2, blocking collectives, merged(): gathered = jax.tree.map(lambda a: lax.all_gather(a, axis), part)  44.3 us
    unnamed x1, blocking collectives  14.5 us
    all_to_all x1, starting transfers between devices, on_device(): lax.all_to_all(request, ('blk', 'grp'), split_axis=0, concat_axis=0, tile...  11.1 us
    all_to_all x1, starting transfers between devices, on_device(): lax.all_to_all(outgoing, ('blk', 'grp'), split_axis=0, concat_axis=0, til...  7.75 us
    all_to_all x1, starting transfers between devices, on_device(): lax.all_to_all(fetched, ('blk', 'grp'), split_axis=0, concat_axis=0, tile...  5.78 us
  transfers between devices with their start and end apart: 20, of which 13 were waited for; matrix products, arithmetic and copies ran while one was open for 13% of the time, Pallas kernels for 0%

commit v1 on v0

v1 whole, which is shorter than its diff:
```python
import jax
import jax.numpy as jnp
from jax import lax
from jax.experimental import pallas as pl
from jax.experimental.pallas import tpu as pltpu
from jax.sharding import PartitionSpec as P

MESH = pl.DeviceIdType.MESH
BF = jnp.bfloat16
F32 = jnp.float32
INV = 50.0
D = 4096
EXT = 128
NEG = 64
ROWS = 16
COLS = NEG + ROWS
CH = 1024
NF = D // CH
FLOOR = -1e30


def kernel(
    q_in, p_in, n_in, e_in, oq, op, on,
    Q, C, S, W, MU, sibs, ownq, rsib, G, rB, T, rA, g3, g12, gsend, g0, rx2, rf1, rf2, st1, st2,
    lsem, sx, rx, sq, rq, sst, rst1, rst2, sg, rg2, rgf1, rgf2, ssib, rsibs, sB, rBs, sA, rAs,
):
    b_id = lax.axis_index("blk")
    g_id = lax.axis_index("grp")
    x = b_id % 4
    y = (g_id // 8) * 2 + b_id // 4
    z = (g_id // 2) % 4
    c = g_id % 2

    def dev(xx, yy, zz, cc):
        xx, yy, zz = (xx + 4) % 4, (yy + 4) % 4, (zz + 4) % 4
        return {"blk": (yy % 2) * 4 + xx, "grp": ((yy // 2) * 4 + zz) * 2 + cc}

    right, left, sib = dev(x + 1, y, z, c), dev(x - 1, y, z, c), dev(x, y, z, 1 - c)
    A = z + c * (y - z)
    B = y + c * (z - y)

    def at(a, b):
        a, b = (a + 4) % 4, (b + 4) % 4
        return dev(x, b + c * (a - b), a + c * (b - a), c)

    def slot(cc, b, a):
        return cc * 16 + ((b + 4) % 4) * 4 + (a + 4) % 4

    def rows_of(s, count=ROWS):
        return pl.ds(pl.multiple_of(s * ROWS, ROWS), count)

    sent = []

    def send(src, dst, ss, rs, to):
        cp = pltpu.make_async_remote_copy(
            src_ref=src, dst_ref=dst, send_sem=ss, recv_sem=rs, device_id=to, device_id_type=MESH
        )
        cp.start()
        sent.append(cp)

    def arrived(dst, rs):
        pltpu.make_async_remote_copy(
            src_ref=dst, dst_ref=dst, send_sem=lsem.at[0], recv_sem=rs, device_id=sib, device_id_type=MESH
        ).wait_recv()

    mine = slot(c, B, A)
    own_rows = rows_of(mine)
    local = [
        pltpu.make_async_copy(n_in, C.at[pl.ds(0, NEG)], lsem.at[0]),
        pltpu.make_async_copy(p_in, C.at[pl.ds(NEG, ROWS)], lsem.at[1]),
        pltpu.make_async_copy(q_in, Q.at[own_rows, pl.ds(0, D)], lsem.at[2]),
        pltpu.make_async_copy(e_in, Q.at[own_rows, pl.ds(D, EXT)], lsem.at[3]),
    ]
    for cp in local:
        cp.start()
    barrier = pltpu.get_barrier_semaphore()
    greet = [right, left, sib]
    greet += [dev(x, y + dy, z, cc) for dy in (1, 2, 3) for cc in (0, 1)]
    greet += [dev(x, y, z + dz, c) for dz in (1, 2, 3)]
    for to in greet:
        pl.semaphore_signal(barrier, inc=1, device_id=to, device_id_type=MESH)
    for cp in local:
        cp.wait()
    pl.semaphore_wait(barrier, len(greet))

    def fcols(f):
        return pl.ds(f * CH, CH)

    def crows(k):
        return pl.ds(k * COLS, COLS)

    for i in range(NF):
        f, h = i, (i + 2) % 4
        send(C.at[crows(0), fcols(f)], C.at[crows(1), fcols(f)], sx.at[0, f], rx.at[0, f], right)
        send(C.at[crows(0), fcols(h)], C.at[crows(2), fcols(h)], sx.at[1, h], rx.at[1, h], left)
    for da in (1, 3, 2):
        send(Q.at[own_rows], Q.at[own_rows], sq.at[0, da], rq.at[mine], at(A + da, B))

    def spread(s):
        da = s
        r = slot(c, B, A - da)
        rr = rows_of(r)
        if da:
            arrived(Q.at[rr], rq.at[r])
        for db in (1, 3, 2):
            send(Q.at[rr], Q.at[rr], sq.at[1 + da, db], rq.at[r], at(A, B + db))
        send(Q.at[rr], Q.at[rr], sq.at[1 + da, 0], rq.at[r], sib)

    for da in (0, 1, 3, 2):
        spread(da)
    for f in (0, 1):
        arrived(C.at[crows(1), fcols(f)], rx.at[0, f])
        send(C.at[crows(1), fcols(f)], C.at[crows(3), fcols(f)], sx.at[2, f], rx.at[2, f], right)
        h = f + 2
        arrived(C.at[crows(2), fcols(h)], rx.at[1, h])
        send(C.at[crows(2), fcols(h)], C.at[crows(3), fcols(h)], sx.at[2, h], rx.at[2, h], left)
    for da in (0, 1, 3, 2):
        for db in (1, 3, 2):
            r = slot(c, B - db, A - da)
            rr = rows_of(r)
            arrived(Q.at[rr], rq.at[r])
            send(Q.at[rr], Q.at[rr], sq.at[4 + db, da], rq.at[r], sib)
    for k in range(16):
        r = (1 - c) * 16 + k
        arrived(Q.at[rows_of(r)], rq.at[r])

    ext = jnp.transpose(Q[:, D : D + EXT].astype(F32))
    ids = ext[0:8] * 128.0 + ext[8:16]
    col_neg = lax.broadcasted_iota(jnp.int32, (NEG, 512), 0)
    col_pas = lax.broadcasted_iota(jnp.int32, (ROWS, 512), 0)
    for k, dx in enumerate((0, 3, 1, 2)):
        lin = ((y % 2) * 4 + (x + dx) % 4) * 16 + g_id
        gid = (col_neg + lin * NEG).astype(F32)
        mult = jnp.zeros((NEG, 512), F32)
        for h in range(7):
            mult = mult + (ids[h : h + 1] == gid).astype(F32)
        MU[k * COLS : k * COLS + NEG, :] = mult
        pid = (col_pas + lin * ROWS).astype(F32)
        MU[k * COLS + NEG : (k + 1) * COLS, :] = (ids[7:8] == pid).astype(F32)

    def scores(lo, hi):
        S[lo:hi, :] = INV * lax.dot_general(
            C[lo:hi, :], Q[:, 0:D], (((1,), (1,)), ((), ())), preferred_element_type=F32
        )
        for k in range(lo // COLS, hi // COLS):
            r0, r1 = k * COLS, k * COLS + NEG
            S[r0:r1, :] = jnp.where(MU[r0:r1, :] > 0.0, S[r0:r1, :], FLOOR)

    for f in (2, 3):
        arrived(C.at[crows(1), fcols(f)], rx.at[0, f])
        arrived(C.at[crows(2), fcols(f - 2)], rx.at[1, f - 2])
    scores(0, 3 * COLS)
    for f in (0, 2, 1, 3):
        arrived(C.at[crows(3), fcols(f)], rx.at[2, f])
    scores(3 * COLS, 4 * COLS)

    s_all = S[...]
    m = jnp.max(s_all, 0, keepdims=True)
    e = jnp.exp(s_all - m)
    tot = jnp.zeros((1, 512), F32)
    for k in range(4):
        r0, r1, r2 = k * COLS, k * COLS + NEG, (k + 1) * COLS
        tot = tot + jnp.sum(e[r0:r1] * MU[r0:r1, :], 0, keepdims=True)
        tot = tot + jnp.sum(e[r1:r2], 0, keepdims=True)
    for j in range(4):
        st1[0, j : j + 1, :] = m[:, j * 128 : (j + 1) * 128]
        st1[0, 4 + j : 5 + j, :] = tot[:, j * 128 : (j + 1) * 128]

    def merge(buf, n):
        top = buf[0, 0:4, :]
        for i in range(1, n):
            top = jnp.maximum(top, buf[i, 0:4, :])
        total = jnp.zeros((4, 128), F32)
        for i in range(n):
            total = total + buf[i, 4:8, :] * jnp.exp(buf[i, 0:4, :] - top)
        return top, total

    for i in range(1, 8):
        dy, dc = i // 2, i % 2
        send(st1.at[0], st1.at[i], sst.at[i], rst1.at[i], dev(x, y + dy, z, (c + dc) % 2))
    for i in range(1, 8):
        arrived(st1.at[i], rst1.at[i])
    top, total = merge(st1, 8)
    st2[0, 0:4, :] = top
    st2[0, 4:8, :] = total
    for i in range(1, 4):
        send(st2.at[0], st2.at[i], sst.at[7 + i], rst2.at[i], dev(x, y, z + i, c))
    for i in range(1, 4):
        arrived(st2.at[i], rst2.at[i])
    top, total = merge(st2, 4)
    lt = top + jnp.log(total)
    log_total = jnp.concatenate([lt[j : j + 1, :] for j in range(4)], 1)

    def weights(k):
        r0, r1, r2 = k * COLS, k * COLS + NEG, (k + 1) * COLS
        hard = jnp.exp(S[r0:r1, :] - log_total).astype(BF).astype(F32) * MU[r0:r1, :]
        W[r0:r1, :] = hard.astype(BF)
        W[r1:r2, :] = (jnp.exp(S[r1:r2, :] - log_total) - MU[r1:r2, :]).astype(BF)

    def col_grad(lo, hi, f):
        return INV * jnp.dot(W[lo:hi, :], Q[:, f * CH : (f + 1) * CH], preferred_element_type=F32)

    weights(3)
    for f in (0, 2, 1, 3):
        g3[:, f * CH : (f + 1) * CH] = col_grad(3 * COLS, 4 * COLS, f).astype(BF)
        to = right if f < 2 else left
        send(g3.at[:, fcols(f)], rx2.at[:, fcols(f)], sg.at[0, f], rg2.at[f], to)
    for k in (0, 1, 2):
        weights(k)

    def query_grad(core, f):
        w = W[:, pl.ds(pl.multiple_of(core * 256, 256), 256)]
        return INV * lax.dot_general(
            w, C[:, f * CH : (f + 1) * CH], (((0,), (0,)), ((), ())), preferred_element_type=F32
        )

    for f in range(NF):
        sibs[:, f * CH : (f + 1) * CH] = query_grad(1 - c, f).astype(BF)
        send(sibs.at[:, fcols(f)], rsib.at[:, fcols(f)], ssib.at[f], rsibs.at[f], sib)
    for f in range(NF):
        cs = slice(f * CH, (f + 1) * CH)
        g12[:, cs] = col_grad(COLS, 3 * COLS, f)
        if f < 2:
            gsend[0:COLS, cs] = g12[0:COLS, cs].astype(BF)
            send(gsend.at[pl.ds(0, COLS), fcols(f)], rf2.at[:, fcols(f)], sg.at[1, f], rgf2.at[f], left)
        else:
            gsend[COLS:, cs] = g12[COLS:, cs].astype(BF)
            send(gsend.at[pl.ds(COLS, COLS), fcols(f)], rf1.at[:, fcols(f)], sg.at[1, f], rgf1.at[f], right)
    for f in range(NF):
        ownq[:, f * CH : (f + 1) * CH] = query_grad(c, f)
    for f in range(NF):
        cs = slice(f * CH, (f + 1) * CH)
        arrived(rsib.at[:, fcols(f)], rsibs.at[f])
        G[:, cs] = (ownq[:, cs] + rsib[:, cs].astype(F32)).astype(BF)
        for db in (2, 1, 3):
            src = G.at[rows_of(slot(0, B + db, 0), 64), fcols(f)]
            send(src, rB.at[db, :, fcols(f)], sB.at[db, f], rBs.at[db, f], at(A, B + db))
    for f in (0, 2, 1, 3):
        cs = slice(f * CH, (f + 1) * CH)
        arrived(rx2.at[:, fcols(f)], rg2.at[f])
        if f < 2:
            gsend[COLS:, cs] = (g12[COLS:, cs] + rx2[:, cs].astype(F32)).astype(BF)
            send(gsend.at[pl.ds(COLS, COLS), fcols(f)], rf1.at[:, fcols(f)], sg.at[2, f], rgf1.at[f], right)
        else:
            gsend[0:COLS, cs] = (g12[0:COLS, cs] + rx2[:, cs].astype(F32)).astype(BF)
            send(gsend.at[pl.ds(0, COLS), fcols(f)], rf2.at[:, fcols(f)], sg.at[2, f], rgf2.at[f], left)
    for f in range(NF):
        g0[:, f * CH : (f + 1) * CH] = col_grad(0, COLS, f)
    for f in range(NF):
        cs = slice(f * CH, (f + 1) * CH)
        t = G[rows_of(slot(0, B, 0), 64), cs].astype(F32)
        for db in (1, 2, 3):
            arrived(rB.at[db, :, fcols(f)], rBs.at[db, f])
            t = t + rB[db, :, cs].astype(F32)
        T[:, cs] = t.astype(BF)
        for da in (2, 1, 3):
            src = T.at[rows_of(slot(0, 0, A + da)), fcols(f)]
            send(src, rA.at[da, :, fcols(f)], sA.at[da, f], rAs.at[da, f], at(A + da, B))
    for f in range(NF):
        cs = slice(f * CH, (f + 1) * CH)
        t = T[rows_of(A), cs].astype(F32)
        for da in (1, 2, 3):
            arrived(rA.at[da, :, fcols(f)], rAs.at[da, f])
            t = t + rA[da, :, cs].astype(F32)
        oq[:, cs] = t.astype(BF)
    for f in (2, 0, 3, 1):
        cs = slice(f * CH, (f + 1) * CH)
        arrived(rf1.at[:, fcols(f)], rgf1.at[f])
        arrived(rf2.at[:, fcols(f)], rgf2.at[f])
        t = g0[:, cs] + rf1[:, cs].astype(F32) + rf2[:, cs].astype(F32)
        on[:, cs] = t[0:NEG].astype(BF)
        op[:, cs] = t[NEG:COLS].astype(BF)
    for cp in sent:
        cp.wait_send()


def on_device(queries, document_vectors, negatives, positives, neg_ids):
    ids = jnp.concatenate([neg_ids, positives[:, None]], 1)
    pad = jnp.zeros((ROWS, EXT - 16), jnp.int32)
    ext = jnp.concatenate([ids // 128, ids % 128, pad], 1).astype(BF)
    dma = pltpu.SemaphoreType.DMA
    vm = pltpu.VMEM
    return pl.pallas_call(
        kernel,
        out_shape=(
            jax.ShapeDtypeStruct((ROWS, D), BF),
            jax.ShapeDtypeStruct((ROWS, D), BF),
            jax.ShapeDtypeStruct((NEG, D), BF),
        ),
        in_specs=[pl.BlockSpec(memory_space=pl.ANY)] * 4,
        out_specs=tuple([pl.BlockSpec(memory_space=pltpu.VMEM)] * 3),
        scratch_shapes=[
            vm((512, D + EXT), BF),
            vm((4 * COLS, D), BF),
            vm((4 * COLS, 512), F32),
            vm((4 * COLS, 512), BF),
            vm((4 * COLS, 512), F32),
            vm((256, D), BF),
            vm((256, D), F32),
            vm((256, D), BF),
            vm((256, D), BF),
            vm((4, 64, D), BF),
            vm((64, D), BF),
            vm((4, ROWS, D), BF),
            vm((COLS, D), BF),
            vm((2 * COLS, D), F32),
            vm((2 * COLS, D), BF),
            vm((COLS, D), F32),
            vm((COLS, D), BF),
            vm((COLS, D), BF),
            vm((COLS, D), BF),
            vm((8, 8, 128), F32),
            vm((4, 8, 128), F32),
            dma((4,)),
            dma((3, NF)),
            dma((3, NF)),
            dma((8, 4)),
            dma((32,)),
            dma((11,)),
            dma((8,)),
            dma((4,)),
            dma((3, NF)),
            dma((NF,)),
            dma((NF,)),
            dma((NF,)),
            dma((NF,)),
            dma((NF,)),
            dma((4, NF)),
            dma((4, NF)),
            dma((4, NF)),
            dma((4, NF)),
        ],
        compiler_params=pltpu.CompilerParams(
            collective_id=0, has_side_effects=True, vmem_limit_bytes=56 * 2**20
        ),
    )(queries, document_vectors, negatives, ext)


def solution(mesh):
    rows = P(("blk", "grp"), None)
    return jax.shard_map(
        on_device,
        mesh=mesh,
        in_specs=(rows, rows, rows, P(("blk", "grp")), rows),
        out_specs=(rows, rows, rows),
        check_vma=False,
    )
```

time: 283 us -> 74.7 us (0.26)
  waiting for transfers between devices: 130 us -> 0 us
  Pallas kernels: 0 us -> 67.7 us
  blocking collectives: 58.8 us -> 0 us
  starting transfers between devices: 28.1 us -> 0 us
  local copies, waits for them, and re-layouts: 28.1 us -> 5.41 us
  between operations: 15.5 us -> 0.67 us
  matrix products: 12.6 us -> 0 us
  other arithmetic: 9.41 us -> 0.76 us
    ppermute x15 -> x0, waiting for transfers between devices: 130 us -> none  [passed_along(): lax.ppermute(array, axis, [(i, (i + by) % peers) for i in range(peers)])]
    pallas_call x0 -> x1, Pallas kernels: none -> 67.7 us  [on_device(): pl.pallas_call(kernel, out_shape=(jax.ShapeDtypeStruct((ROWS, D), BF), ja...]
    all_gather x2 -> x0, blocking collectives: 44.3 us -> none  [merged(): gathered = jax.tree.map(lambda a: lax.all_gather(a, axis), part)]
    all_to_all x3 -> x0, starting transfers between devices: 24.7 us -> none  [the longest x1 11.1 us: on_device(): lax.all_to_all(request, ('blk', 'grp'), split_axis=0, concat_axis=0, tile...]
    reshape x7 -> x0, local copies, waits for them, and re-layouts: 14.8 us -> none  [the longest x1 4.39 us: on_device(): outgoing = outgoing.reshape(devices, capacity, feat_width)]
    unnamed x1 -> x0, blocking collectives: 14.5 us -> none
    dot_general x13 -> x0, matrix products: 12.6 us -> none  [the longest x1 3.41 us: on_device(): jnp.dot(selected_rows, candidate_passages, preferred_element_type=jnp.flo...]
    scatter x1 -> x0, other arithmetic: 4.53 us -> none  [on_device(): outgoing = jnp.zeros((devices * capacity, feat_width), jnp.bfloat16).at[p...]
  transfers between devices with their start and end apart: 20 -> 0, of which waited for: 13 -> 0; matrix products, arithmetic and copies ran while one was open for 13% -> 0% of each run, Pallas kernels for 0% -> 0%
where the time goes in v1:
time: 74.7 us; the launch traced here: 74.5 us
  Pallas kernels  67.7 us (91%)
  local copies, waits for them, and re-layouts  5.41 us (7%)
  other arithmetic  0.76 us (1%)
    pallas_call x1, Pallas kernels, on_device(): pl.pallas_call(kernel, out_shape=(jax.ShapeDtypeStruct((ROWS, D), BF), ja...  67.7 us
    unnamed x10, local copies, waits for them, and re-layouts  5.25 us

profile of v1, /device:TPU:0, one launch (start us, length us, event | category | flops | bytes accessed | tf_op | source)
XLA Modules:
  0.0 74.5 jit_solution(7736645963151464608)
XLA Ops:
  0.6 0.0 copy-start.2
  0.7 0.1 pad.2.clone
  0.7 0.6 copy-done.2
  1.3 0.0 copy-start.1
  1.3 0.1 copy.9
  1.4 0.6 copy-done.1
  2.0 0.1 copy.8
  2.1 0.1 fusion
  2.2 0.7 maximum_maximum_fusion.e_in
  2.8 67.7 %shard_map.76 = (bf16[16,4096]{1,0:T(8,128)(2,1)}, bf16[16,4096]{1,0:T(8,128)(2,1)}, bf16[64,4096]{1,0:T(8,128)(2,1)}) custom-call(bf16[16,4096]{1,0:T(8,128)(2,1)} %q_in.1, bf16[16,4096]{1,0:T(8,128)(2,1)} %p_in.1, bf16[64,4096]{1,0:T(8,128)(2,1)} %n_in.1, bf16[16,128]{1,0:T(8,128)(2,1)} %maximum_maximum_fusion.e_in), custom_call_target="tpu_custom_call" | custom-call | tf_op jit(solution)/shard_map/pallas_call | solution.py:283
  70.5 0.0 copy-start
  70.5 1.6 %copy.13 = bf16[16,4096]{1,0:T(8,128)(2,1)} copy(bf16[16,4096]{1,0:T(8,128)(2,1)} %get-tuple-element.8) | data formatting | bytes 262144
  72.2 1.6 %copy.14 = bf16[16,4096]{1,0:T(8,128)(2,1)} copy(bf16[16,4096]{1,0:T(8,128)(2,1)} %get-tuple-element.9) | data formatting | bytes 262144
  73.7 0.0 copy-done
  73.7 0.8 %copy.15 = bf16[64,4096]{1,0:T(8,128)(2,1)} copy(bf16[64,4096]{1,0:T(8,128)(2,1)S(1)} %copy-done) | data formatting | bytes 1048576
  (1 shorter events, 0.0 us)
Async XLA Ops:
  0.6 0.7 copy-start.2
  1.3 0.7 copy-start.1
  70.5 3.2 %copy-start = (bf16[64,4096]{1,0:T(8,128)(2,1)S(1)}, bf16[64,4096]{1,0:T(8,128)(2,1)}, u32[]{:S(2)}) copy-start(bf16[64,4096]{1,0:T(8,128)(2,1)} %get-tuple-element.10) | copy-start | bytes 1572868

commit v2 on v1

--- a/solution.py
+++ b/solution.py
@@ -20,9 +20,9 @@
 
 
 def kernel(
-    q_in, p_in, n_in, e_in, oq, op, on,
-    Q, C, S, W, MU, sibs, ownq, rsib, G, rB, T, rA, g3, g12, gsend, g0, rx2, rf1, rf2, st1, st2,
-    lsem, sx, rx, sq, rq, sst, rst1, rst2, sg, rg2, rgf1, rgf2, ssib, rsibs, sB, rBs, sA, rAs,
+    q_in, p_in, n_in, pos_in, ids_in, out,
+    PO, ID, E, Q, C, S, W, MU, sibs, ownq, rsib, G, rB2, gB, rB, T, rA, g3, g12, gsend, g0, rx2, rf1, rf2, st1, st2,
+    lsem, sx, rx, sq, ssq, rq, sst, rst1, rst2, sg, rg2, rgf1, rgf2, ssib, rsibs, sB, rB2s, rBs, sA, rAs,
 ):
     b_id = lax.axis_index("blk")
     g_id = lax.axis_index("grp")
@@ -69,18 +69,25 @@
         pltpu.make_async_copy(n_in, C.at[pl.ds(0, NEG)], lsem.at[0]),
         pltpu.make_async_copy(p_in, C.at[pl.ds(NEG, ROWS)], lsem.at[1]),
         pltpu.make_async_copy(q_in, Q.at[own_rows, pl.ds(0, D)], lsem.at[2]),
-        pltpu.make_async_copy(e_in, Q.at[own_rows, pl.ds(D, EXT)], lsem.at[3]),
+        pltpu.make_async_copy(pos_in, PO, lsem.at[3]),
+        pltpu.make_async_copy(ids_in, ID, lsem.at[4]),
     ]
     for cp in local:
         cp.start()
     barrier = pltpu.get_barrier_semaphore()
-    greet = [right, left, sib]
-    greet += [dev(x, y + dy, z, cc) for dy in (1, 2, 3) for cc in (0, 1)]
-    greet += [dev(x, y, z + dz, c) for dz in (1, 2, 3)]
+    greet = [dev(x, y + dy, z, cc) for dy in (2, 1, 3) for cc in (0, 1)]
+    greet += [dev(x, y, z + dz, c) for dz in (2, 1, 3)]
+    greet += [right, left, sib]
     for to in greet:
         pl.semaphore_signal(barrier, inc=1, device_id=to, device_id_type=MESH)
+    E[...] = jnp.zeros((128, 128), F32)
     for cp in local:
         cp.wait()
+    for r, part in ((0, ID[...]), (7, PO[...])):
+        n = part.shape[0]
+        E[r : r + n, 0:ROWS] = (part // 128).astype(F32)
+        E[8 + r : 8 + r + n, 0:ROWS] = (part % 128).astype(F32)
+    Q[own_rows, D : D + EXT] = jnp.transpose(E[...])[0:ROWS].astype(BF)
     pl.semaphore_wait(barrier, len(greet))
 
     def fcols(f):
@@ -96,30 +103,47 @@
     for da in (1, 3, 2):
         send(Q.at[own_rows], Q.at[own_rows], sq.at[0, da], rq.at[mine], at(A + da, B))
 
-    def spread(s):
-        da = s
+    def to_sib(r, i):
+        send(Q.at[rows_of(r)], Q.at[rows_of(r)], ssq.at[i], rq.at[r], sib)
+
+    def spread(da):
         r = slot(c, B, A - da)
         rr = rows_of(r)
         if da:
             arrived(Q.at[rr], rq.at[r])
-        for db in (1, 3, 2):
-            send(Q.at[rr], Q.at[rr], sq.at[1 + da, db], rq.at[r], at(A, B + db))
-        send(Q.at[rr], Q.at[rr], sq.at[1 + da, 0], rq.at[r], sib)
-
-    for da in (0, 1, 3, 2):
-        spread(da)
-    for f in (0, 1):
+        for i, db in enumerate((1, -1)):
+            send(Q.at[rr], Q.at[rr], sq.at[1 + i, da], rq.at[r], at(A, B + db))
+        to_sib(r, da)
+
+    def pass_on(da):
+        for i, db in enumerate((1, -1)):
+            r = slot(c, B - db, A - da)
+            rr = rows_of(r)
+            arrived(Q.at[rr], rq.at[r])
+            if da % 2 == i:
+                send(Q.at[rr], Q.at[rr], sq.at[3, da], rq.at[r], at(A, B + db))
+            to_sib(r, 4 + 4 * i + da)
+
+    def columns_on(f):
         arrived(C.at[crows(1), fcols(f)], rx.at[0, f])
         send(C.at[crows(1), fcols(f)], C.at[crows(3), fcols(f)], sx.at[2, f], rx.at[2, f], right)
         h = f + 2
         arrived(C.at[crows(2), fcols(h)], rx.at[1, h])
         send(C.at[crows(2), fcols(h)], C.at[crows(3), fcols(h)], sx.at[2, h], rx.at[2, h], left)
+
+    for da in (0, 1, 3):
+        spread(da)
+    pass_on(0)
+    spread(2)
+    columns_on(0)
+    pass_on(1)
+    pass_on(3)
+    columns_on(1)
+    pass_on(2)
     for da in (0, 1, 3, 2):
-        for db in (1, 3, 2):
-            r = slot(c, B - db, A - da)
-            rr = rows_of(r)
-            arrived(Q.at[rr], rq.at[r])
-            send(Q.at[rr], Q.at[rr], sq.at[4 + db, da], rq.at[r], sib)
+        r = slot(c, B + 2, A - da)
+        arrived(Q.at[rows_of(r)], rq.at[r])
+        to_sib(r, 12 + da)
     for k in range(16):
         r = (1 - c) * 16 + k
         arrived(Q.at[rows_of(r)], rq.at[r])
@@ -138,30 +162,37 @@
         pid = (col_pas + lin * ROWS).astype(F32)
         MU[k * COLS + NEG : (k + 1) * COLS, :] = (ids[7:8] == pid).astype(F32)
 
-    def scores(lo, hi):
-        S[lo:hi, :] = INV * lax.dot_general(
-            C[lo:hi, :], Q[:, 0:D], (((1,), (1,)), ((), ())), preferred_element_type=F32
+    def dots(lo, hi, d0, d1):
+        return lax.dot_general(
+            C[lo:hi, d0:d1], Q[:, d0:d1], (((1,), (1,)), ((), ())), preferred_element_type=F32
         )
+
+    def partial_stats(lo, hi):
         for k in range(lo // COLS, hi // COLS):
             r0, r1 = k * COLS, k * COLS + NEG
             S[r0:r1, :] = jnp.where(MU[r0:r1, :] > 0.0, S[r0:r1, :], FLOOR)
+        m = jnp.max(S[lo:hi, :], 0, keepdims=True)
+        tot = jnp.zeros((1, 512), F32)
+        for k in range(lo // COLS, hi // COLS):
+            r0, r1, r2 = k * COLS, k * COLS + NEG, (k + 1) * COLS
+            tot = tot + jnp.sum(jnp.exp(S[r0:r1, :] - m) * MU[r0:r1, :], 0, keepdims=True)
+            tot = tot + jnp.sum(jnp.exp(S[r1:r2, :] - m), 0, keepdims=True)
+        return m, tot
 
     for f in (2, 3):
         arrived(C.at[crows(1), fcols(f)], rx.at[0, f])
         arrived(C.at[crows(2), fcols(f - 2)], rx.at[1, f - 2])
-    scores(0, 3 * COLS)
+    S[0 : 3 * COLS, :] = INV * dots(0, 3 * COLS, 0, D)
+    m_a, tot_a = partial_stats(0, 3 * COLS)
+    acc = jnp.zeros((COLS, 512), F32)
     for f in (0, 2, 1, 3):
         arrived(C.at[crows(3), fcols(f)], rx.at[2, f])
-    scores(3 * COLS, 4 * COLS)
-
-    s_all = S[...]
-    m = jnp.max(s_all, 0, keepdims=True)
-    e = jnp.exp(s_all - m)
-    tot = jnp.zeros((1, 512), F32)
-    for k in range(4):
-        r0, r1, r2 = k * COLS, k * COLS + NEG, (k + 1) * COLS
-        tot = tot + jnp.sum(e[r0:r1] * MU[r0:r1, :], 0, keepdims=True)
-        tot = tot + jnp.sum(e[r1:r2], 0, keepdims=True)
+        acc = acc + dots(3 * COLS, 4 * COLS, f * CH, (f + 1) * CH)
+    S[3 * COLS : 4 * COLS, :] = INV * acc
+    m_b, tot_b = partial_stats(3 * COLS, 4 * COLS)
+
+    m = jnp.maximum(m_a, m_b)
+    tot = tot_a * jnp.exp(m_a - m) + tot_b * jnp.exp(m_b - m)
     for j in range(4):
         st1[0, j : j + 1, :] = m[:, j * 128 : (j + 1) * 128]
         st1[0, 4 + j : 5 + j, :] = tot[:, j * 128 : (j + 1) * 128]
@@ -214,6 +245,12 @@
             w, C[:, f * CH : (f + 1) * CH], (((0,), (0,)), ((), ())), preferred_element_type=F32
         )
 
+    def half(i):
+        return pl.ds(32 * i, 32)
+
+    def group(b, i):
+        return rows_of(slot(0, b, 2 * i), 32)
+
     for f in range(NF):
         sibs[:, f * CH : (f + 1) * CH] = query_grad(1 - c, f).astype(BF)
         send(sibs.at[:, fcols(f)], rsib.at[:, fcols(f)], ssib.at[f], rsibs.at[f], sib)
@@ -232,9 +269,20 @@
         cs = slice(f * CH, (f + 1) * CH)
         arrived(rsib.at[:, fcols(f)], rsibs.at[f])
         G[:, cs] = (ownq[:, cs] + rsib[:, cs].astype(F32)).astype(BF)
-        for db in (2, 1, 3):
-            src = G.at[rows_of(slot(0, B + db, 0), 64), fcols(f)]
-            send(src, rB.at[db, :, fcols(f)], sB.at[db, f], rBs.at[db, f], at(A, B + db))
+        for i, db in enumerate((1, -1)):
+            h, o = half(i), half(1 - i)
+            src = G.at[group(B + 2, i), fcols(f)]
+            send(src, rB2.at[h, fcols(f)], sB.at[0, i, f], rB2s.at[i, f], at(A, B + db))
+            src = G.at[group(B + db, 1 - i), fcols(f)]
+            send(src, rB.at[i, o, fcols(f)], sB.at[1, i, f], rBs.at[i, 1 - i, f], at(A, B + db))
+    for f in range(NF):
+        cs = slice(f * CH, (f + 1) * CH)
+        for i, db in enumerate((1, -1)):
+            h = half(i)
+            arrived(rB2.at[h, fcols(f)], rB2s.at[i, f])
+            t = G[group(B + db, i), cs].astype(F32) + rB2[h, cs].astype(F32)
+            gB[h, cs] = t.astype(BF)
+            send(gB.at[h, fcols(f)], rB.at[i, h, fcols(f)], sB.at[2, i, f], rBs.at[i, i, f], at(A, B + db))
     for f in (0, 2, 1, 3):
         cs = slice(f * CH, (f + 1) * CH)
         arrived(rx2.at[:, fcols(f)], rg2.at[f])
@@ -249,9 +297,10 @@
     for f in range(NF):
         cs = slice(f * CH, (f + 1) * CH)
         t = G[rows_of(slot(0, B, 0), 64), cs].astype(F32)
-        for db in (1, 2, 3):
-            arrived(rB.at[db, :, fcols(f)], rBs.at[db, f])
-            t = t + rB[db, :, cs].astype(F32)
+        for i in range(2):
+            for j in range(2):
+                arrived(rB.at[i, half(j), fcols(f)], rBs.at[i, j, f])
+            t = t + rB[i, :, cs].astype(F32)
         T[:, cs] = t.astype(BF)
         for da in (2, 1, 3):
             src = T.at[rows_of(slot(0, 0, A + da)), fcols(f)]
@@ -262,34 +311,33 @@
         for da in (1, 2, 3):
             arrived(rA.at[da, :, fcols(f)], rAs.at[da, f])
             t = t + rA[da, :, cs].astype(F32)
-        oq[:, cs] = t.astype(BF)
+        out[0:ROWS, cs] = t.astype(BF)
     for f in (2, 0, 3, 1):
         cs = slice(f * CH, (f + 1) * CH)
         arrived(rf1.at[:, fcols(f)], rgf1.at[f])
         arrived(rf2.at[:, fcols(f)], rgf2.at[f])
         t = g0[:, cs] + rf1[:, cs].astype(F32) + rf2[:, cs].astype(F32)
-        on[:, cs] = t[0:NEG].astype(BF)
-        op[:, cs] = t[NEG:COLS].astype(BF)
+        out[2 * ROWS :, cs] = t[0:NEG].astype(BF)
+        out[ROWS : 2 * ROWS, cs] = t[NEG:COLS].astype(BF)
     for cp in sent:
         cp.wait_send()
 
 
 def on_device(queries, document_vectors, negatives, positives, neg_ids):
-    ids = jnp.concatenate([neg_ids, positives[:, None]], 1)
-    pad = jnp.zeros((ROWS, EXT - 16), jnp.int32)
-    ext = jnp.concatenate([ids // 128, ids % 128, pad], 1).astype(BF)
     dma = pltpu.SemaphoreType.DMA
     vm = pltpu.VMEM
-    return pl.pallas_call(
+    hbm = [
+        pltpu.with_memory_space_constraint(a, pltpu.HBM)
+        for a in (queries, document_vectors, negatives, positives.reshape(1, ROWS), neg_ids.T)
+    ]
+    out = pl.pallas_call(
         kernel,
-        out_shape=(
-            jax.ShapeDtypeStruct((ROWS, D), BF),
-            jax.ShapeDtypeStruct((ROWS, D), BF),
-            jax.ShapeDtypeStruct((NEG, D), BF),
-        ),
-        in_specs=[pl.BlockSpec(memory_space=pl.ANY)] * 4,
-        out_specs=tuple([pl.BlockSpec(memory_space=pltpu.VMEM)] * 3),
+        out_shape=pltpu.VMEM((2 * ROWS + NEG, D), BF),
+        in_specs=[pl.BlockSpec(memory_space=pltpu.HBM)] * 5,
         scratch_shapes=[
+            vm((1, ROWS), jnp.int32),
+            vm((7, ROWS), jnp.int32),
+            vm((128, 128), F32),
             vm((512, D + EXT), BF),
             vm((4 * COLS, D), BF),
             vm((4 * COLS, 512), F32),
@@ -299,7 +347,9 @@
             vm((256, D), F32),
             vm((256, D), BF),
             vm((256, D), BF),
-            vm((4, 64, D), BF),
+            vm((64, D), BF),
+            vm((64, D), BF),
+            vm((2, 64, D), BF),
             vm((64, D), BF),
             vm((4, ROWS, D), BF),
             vm((COLS, D), BF),
@@ -311,10 +361,11 @@
             vm((COLS, D), BF),
             vm((8, 8, 128), F32),
             vm((4, 8, 128), F32),
-            dma((4,)),
+            dma((5,)),
             dma((3, NF)),
             dma((3, NF)),
-            dma((8, 4)),
+            dma((4, 4)),
+            dma((16,)),
             dma((32,)),
             dma((11,)),
             dma((8,)),
@@ -325,15 +376,17 @@
             dma((NF,)),
             dma((NF,)),
             dma((NF,)),
-            dma((4, NF)),
-            dma((4, NF)),
+            dma((3, 2, NF)),
+            dma((2, NF)),
+            dma((2, 2, NF)),
             dma((4, NF)),
             dma((4, NF)),
         ],
         compiler_params=pltpu.CompilerParams(
-            collective_id=0, has_side_effects=True, vmem_limit_bytes=56 * 2**20
+            collective_id=0, has_side_effects=True, vmem_limit_bytes=44 * 2**20
         ),
-    )(queries, document_vectors, negatives, ext)
+    )(*hbm)
+    return out[0:ROWS], out[ROWS : 2 * ROWS], out[2 * ROWS :]
 
 
 def solution(mesh):

time: 74.7 us -> 65.8 us (0.88)
  Pallas kernels: 67.7 us -> 63.5 us
  local copies, waits for them, and re-layouts: 5.41 us -> 1.54 us
  other arithmetic: 0.76 us -> 0 us
    unnamed x10 -> x0, local copies, waits for them, and re-layouts: 5.25 us -> none
    pallas_call x1, Pallas kernels: 67.7 us -> 63.5 us  [on_device(): pl.pallas_call(kernel, out_shape=pltpu.VMEM((2 * ROWS + NEG, D), BF), in_...]
    slice x0 -> x2, local copies, waits for them, and re-layouts: none -> 1.54 us  [on_device(): return (out[0:ROWS], out[ROWS:2 * ROWS], out[2 * ROWS:])]
where the time goes in v2:
time: 65.8 us; the launch traced here: 65.7 us
  Pallas kernels  63.5 us (97%)
  local copies, waits for them, and re-layouts  1.54 us (2%)
    pallas_call x1, Pallas kernels, on_device(): pl.pallas_call(kernel, out_shape=pltpu.VMEM((2 * ROWS + NEG, D), BF), in_...  63.5 us
    slice x2, local copies, waits for them, and re-layouts, on_device(): return (out[0:ROWS], out[ROWS:2 * ROWS], out[2 * ROWS:])  1.54 us

profile of v2, /device:TPU:0, one launch (start us, length us, event | category | flops | bytes accessed | tf_op | source)
XLA Modules:
  0.0 65.7 jit_solution(14958000881908275984)
XLA Ops:
  0.6 63.5 %shard_map.76 = bf16[96,4096]{1,0:T(8,128)(2,1)S(1)} custom-call(bf16[16,4096]{1,0:T(8,128)(2,1)} %q_in.1, bf16[16,4096]{1,0:T(8,128)(2,1)} %p_in.1, bf16[64,4096]{1,0:T(8,128)(2,1)} %n_in.1, s32[1,16]{1,0:T(1,128)} %bitcast.3, s32[7,16]{1,0:T(8,128)} %bitcast.2), custom_call_target="tpu_custom_call" | custom-call | tf_op jit(solution)/shard_map/pallas_call | solution.py:333
  64.1 0.7 %fusion = (bf16[16,4096]{1,0:T(8,128)(2,1)}, bf16[16,4096]{1,0:T(8,128)(2,1)}) fusion(bf16[96,4096]{1,0:T(8,128)(2,1)S(1)} %shard_map.76), kind=kLoop, calls=%fused_computation | loop fusion | bytes 524288 | tf_op jit(solution)/shard_map/slice | solution.py:389
  64.8 0.8 %slice.11 = bf16[64,4096]{1,0:T(8,128)(2,1)} slice(bf16[96,4096]{1,0:T(8,128)(2,1)S(1)} %shard_map.76), slice={[32:96], [0:4096]} | slice | bytes 1048576 | tf_op jit(solution)/shard_map/slice | solution.py:389

commit v3 on v2

--- a/solution.py
+++ b/solution.py
@@ -21,8 +21,8 @@
 
 def kernel(
     q_in, p_in, n_in, pos_in, ids_in, out,
-    PO, ID, E, Q, C, S, W, MU, sibs, ownq, rsib, G, rB2, gB, rB, T, rA, g3, g12, gsend, g0, rx2, rf1, rf2, st1, st2,
-    lsem, sx, rx, sq, ssq, rq, sst, rst1, rst2, sg, rg2, rgf1, rgf2, ssib, rsibs, sB, rB2s, rBs, sA, rAs,
+    PO, ID, E, Q, C, S, W, MU, sibs, ownq, rsib, G, rB2, gB, rB, T, rA, g3, g12, gsend, g0, rx2, rf1, rf2, st1,
+    lsem, sx, rx, sq, ssq, rq, sst, rst1, sg, rg2, rgf1, rgf2, ssib, rsibs, sB, rB2s, rBs, sA, rAs,
 ):
     b_id = lax.axis_index("blk")
     g_id = lax.axis_index("grp")
@@ -206,19 +206,12 @@
             total = total + buf[i, 4:8, :] * jnp.exp(buf[i, 0:4, :] - top)
         return top, total
 
-    for i in range(1, 8):
-        dy, dc = i // 2, i % 2
-        send(st1.at[0], st1.at[i], sst.at[i], rst1.at[i], dev(x, y + dy, z, (c + dc) % 2))
-    for i in range(1, 8):
+    for i in (*range(16, 24), *range(8, 16), *range(24, 32), *range(1, 8)):
+        dy, dz, dc = i // 8, i // 2 % 4, i % 2
+        send(st1.at[0], st1.at[i], sst.at[i], rst1.at[i], dev(x, y + dy, z + dz, (c + dc) % 2))
+    for i in range(1, 32):
         arrived(st1.at[i], rst1.at[i])
-    top, total = merge(st1, 8)
-    st2[0, 0:4, :] = top
-    st2[0, 4:8, :] = total
-    for i in range(1, 4):
-        send(st2.at[0], st2.at[i], sst.at[7 + i], rst2.at[i], dev(x, y, z + i, c))
-    for i in range(1, 4):
-        arrived(st2.at[i], rst2.at[i])
-    top, total = merge(st2, 4)
+    top, total = merge(st1, 32)
     lt = top + jnp.log(total)
     log_total = jnp.concatenate([lt[j : j + 1, :] for j in range(4)], 1)
 
@@ -359,17 +352,15 @@
             vm((COLS, D), BF),
             vm((COLS, D), BF),
             vm((COLS, D), BF),
-            vm((8, 8, 128), F32),
-            vm((4, 8, 128), F32),
+            vm((32, 8, 128), F32),
             dma((5,)),
             dma((3, NF)),
             dma((3, NF)),
             dma((4, 4)),
             dma((16,)),
             dma((32,)),
-            dma((11,)),
-            dma((8,)),
-            dma((4,)),
+            dma((32,)),
+            dma((32,)),
             dma((3, NF)),
             dma((NF,)),
             dma((NF,)),

time: 65.8 us -> 64.4 us (0.979)
  Pallas kernels: 63.5 us -> 61.8 us
    pallas_call x1, Pallas kernels: 63.5 us -> 61.8 us  [on_device(): pl.pallas_call(kernel, out_shape=pltpu.VMEM((2 * ROWS + NEG, D), BF), in_...]
where the time goes in v3:
time: 64.4 us; the launch traced here: 63.9 us
  Pallas kernels  61.8 us (96%)
  local copies, waits for them, and re-layouts  1.54 us (2%)
    pallas_call x1, Pallas kernels, on_device(): pl.pallas_call(kernel, out_shape=pltpu.VMEM((2 * ROWS + NEG, D), BF), in_...  61.8 us
    slice x2, local copies, waits for them, and re-layouts, on_device(): return (out[0:ROWS], out[ROWS:2 * ROWS], out[2 * ROWS:])  1.54 us

profile of v3, /device:TPU:0, one launch (start us, length us, event | category | flops | bytes accessed | tf_op | source)
XLA Modules:
  0.0 63.9 jit_solution(18096854574505901155)
XLA Ops:
  0.6 61.8 %shard_map.76 = bf16[96,4096]{1,0:T(8,128)(2,1)S(1)} custom-call(bf16[16,4096]{1,0:T(8,128)(2,1)} %q_in.1, bf16[16,4096]{1,0:T(8,128)(2,1)} %p_in.1, bf16[64,4096]{1,0:T(8,128)(2,1)} %n_in.1, s32[1,16]{1,0:T(1,128)} %bitcast.3, s32[7,16]{1,0:T(8,128)} %bitcast.2), custom_call_target="tpu_custom_call" | custom-call | tf_op jit(solution)/shard_map/pallas_call | solution.py:326
  62.4 0.7 %fusion = (bf16[16,4096]{1,0:T(8,128)(2,1)}, bf16[16,4096]{1,0:T(8,128)(2,1)}) fusion(bf16[96,4096]{1,0:T(8,128)(2,1)S(1)} %shard_map.76), kind=kLoop, calls=%fused_computation | loop fusion | bytes 524288 | tf_op jit(solution)/shard_map/slice | solution.py:380
  63.1 0.8 %slice.11 = bf16[64,4096]{1,0:T(8,128)(2,1)} slice(bf16[96,4096]{1,0:T(8,128)(2,1)S(1)} %shard_map.76), slice={[32:96], [0:4096]} | slice | bytes 1048576 | tf_op jit(solution)/shard_map/slice | solution.py:380

commit v4 on v3

--- a/solution.py
+++ b/solution.py
@@ -21,7 +21,7 @@
 
 def kernel(
     q_in, p_in, n_in, pos_in, ids_in, out,
-    PO, ID, E, Q, C, S, W, MU, sibs, ownq, rsib, G, rB2, gB, rB, T, rA, g3, g12, gsend, g0, rx2, rf1, rf2, st1,
+    PO, ID, E, Q, C, S, W, MU, sibs, ownq, rsib, G, rB2, gB, rB, T, rA, g3, g12, gsend, g0, rx2, rf1, rf2, st1, MT,
     lsem, sx, rx, sq, ssq, rq, sst, rst1, sg, rg2, rgf1, rgf2, ssib, rsibs, sB, rB2s, rBs, sA, rAs,
 ):
     b_id = lax.axis_index("blk")
@@ -57,6 +57,11 @@
         )
         cp.start()
         sent.append(cp)
+
+    def flush():
+        for cp in sent:
+            cp.wait_send()
+        sent.clear()
 
     def arrived(dst, rs):
         pltpu.make_async_remote_copy(
@@ -75,9 +80,7 @@
     for cp in local:
         cp.start()
     barrier = pltpu.get_barrier_semaphore()
-    greet = [dev(x, y + dy, z, cc) for dy in (2, 1, 3) for cc in (0, 1)]
-    greet += [dev(x, y, z + dz, c) for dz in (2, 1, 3)]
-    greet += [right, left, sib]
+    greet = [at(A + 2, B), at(A, B + 2), at(A + 1, B), at(A - 1, B), at(A, B + 1), at(A, B - 1), right, left, sib]
     for to in greet:
         pl.semaphore_signal(barrier, inc=1, device_id=to, device_id_type=MESH)
     E[...] = jnp.zeros((128, 128), F32)
@@ -113,6 +116,8 @@
             arrived(Q.at[rr], rq.at[r])
         for i, db in enumerate((1, -1)):
             send(Q.at[rr], Q.at[rr], sq.at[1 + i, da], rq.at[r], at(A, B + db))
+        if da > 1:
+            send(Q.at[rr], Q.at[rr], sq.at[3, da], rq.at[r], at(A, B + 2))
         to_sib(r, da)
 
     def pass_on(da):
@@ -120,7 +125,7 @@
             r = slot(c, B - db, A - da)
             rr = rows_of(r)
             arrived(Q.at[rr], rq.at[r])
-            if da % 2 == i:
+            if da == i:
                 send(Q.at[rr], Q.at[rr], sq.at[3, da], rq.at[r], at(A, B + db))
             to_sib(r, 4 + 4 * i + da)
 
@@ -144,52 +149,59 @@
         r = slot(c, B + 2, A - da)
         arrived(Q.at[rows_of(r)], rq.at[r])
         to_sib(r, 12 + da)
+    col_neg = lax.broadcasted_iota(jnp.int32, (NEG, 256), 0)
+    col_pas = lax.broadcasted_iota(jnp.int32, (ROWS, 256), 0)
+
+    def dots(lo, hi, rows, d0, d1):
+        return INV * lax.dot_general(
+            C[lo:hi, d0:d1], Q[rows, d0:d1], (((1,), (1,)), ((), ())), preferred_element_type=F32
+        )
+
+    def partial_stats(lo, hi, qs):
+        for k in range(lo // COLS, hi // COLS):
+            r0, r1 = k * COLS, k * COLS + NEG
+            S[r0:r1, qs] = jnp.where(MU[r0:r1, qs] > 0.0, S[r0:r1, qs], FLOOR)
+        m = jnp.max(S[lo:hi, qs], 0, keepdims=True)
+        tot = jnp.zeros_like(m)
+        for k in range(lo // COLS, hi // COLS):
+            r0, r1, r2 = k * COLS, k * COLS + NEG, (k + 1) * COLS
+            tot = tot + jnp.sum(jnp.exp(S[r0:r1, qs] - m) * MU[r0:r1, qs], 0, keepdims=True)
+            tot = tot + jnp.sum(jnp.exp(S[r1:r2, qs] - m), 0, keepdims=True)
+        return m, tot
+
+    def half_scores(core):
+        qs = pl.ds(pl.multiple_of(core * 256, 256), 256)
+        ext = jnp.transpose(Q[qs, D : D + EXT].astype(F32))
+        ids = ext[0:8] * 128.0 + ext[8:16]
+        for k, dx in enumerate((0, 3, 1, 2)):
+            lin = ((y % 2) * 4 + (x + dx) % 4) * 16 + g_id
+            gid = (col_neg + lin * NEG).astype(F32)
+            mult = jnp.zeros((NEG, 256), F32)
+            for h in range(7):
+                mult = mult + (ids[h : h + 1] == gid).astype(F32)
+            MU[k * COLS : k * COLS + NEG, qs] = mult
+            pid = (col_pas + lin * ROWS).astype(F32)
+            MU[k * COLS + NEG : (k + 1) * COLS, qs] = (ids[7:8] == pid).astype(F32)
+        S[0 : 3 * COLS, qs] = dots(0, 3 * COLS, qs, 0, D)
+        m, tot = partial_stats(0, 3 * COLS, qs)
+        MT[0:1, qs] = m
+        MT[1:2, qs] = tot
+
+    for f in (2, 3):
+        arrived(C.at[crows(1), fcols(f)], rx.at[0, f])
+        arrived(C.at[crows(2), fcols(f - 2)], rx.at[1, f - 2])
+    half_scores(c)
     for k in range(16):
         r = (1 - c) * 16 + k
         arrived(Q.at[rows_of(r)], rq.at[r])
-
-    ext = jnp.transpose(Q[:, D : D + EXT].astype(F32))
-    ids = ext[0:8] * 128.0 + ext[8:16]
-    col_neg = lax.broadcasted_iota(jnp.int32, (NEG, 512), 0)
-    col_pas = lax.broadcasted_iota(jnp.int32, (ROWS, 512), 0)
-    for k, dx in enumerate((0, 3, 1, 2)):
-        lin = ((y % 2) * 4 + (x + dx) % 4) * 16 + g_id
-        gid = (col_neg + lin * NEG).astype(F32)
-        mult = jnp.zeros((NEG, 512), F32)
-        for h in range(7):
-            mult = mult + (ids[h : h + 1] == gid).astype(F32)
-        MU[k * COLS : k * COLS + NEG, :] = mult
-        pid = (col_pas + lin * ROWS).astype(F32)
-        MU[k * COLS + NEG : (k + 1) * COLS, :] = (ids[7:8] == pid).astype(F32)
-
-    def dots(lo, hi, d0, d1):
-        return lax.dot_general(
-            C[lo:hi, d0:d1], Q[:, d0:d1], (((1,), (1,)), ((), ())), preferred_element_type=F32
-        )
-
-    def partial_stats(lo, hi):
-        for k in range(lo // COLS, hi // COLS):
-            r0, r1 = k * COLS, k * COLS + NEG
-            S[r0:r1, :] = jnp.where(MU[r0:r1, :] > 0.0, S[r0:r1, :], FLOOR)
-        m = jnp.max(S[lo:hi, :], 0, keepdims=True)
-        tot = jnp.zeros((1, 512), F32)
-        for k in range(lo // COLS, hi // COLS):
-            r0, r1, r2 = k * COLS, k * COLS + NEG, (k + 1) * COLS
-            tot = tot + jnp.sum(jnp.exp(S[r0:r1, :] - m) * MU[r0:r1, :], 0, keepdims=True)
-            tot = tot + jnp.sum(jnp.exp(S[r1:r2, :] - m), 0, keepdims=True)
-        return m, tot
-
-    for f in (2, 3):
-        arrived(C.at[crows(1), fcols(f)], rx.at[0, f])
-        arrived(C.at[crows(2), fcols(f - 2)], rx.at[1, f - 2])
-    S[0 : 3 * COLS, :] = INV * dots(0, 3 * COLS, 0, D)
-    m_a, tot_a = partial_stats(0, 3 * COLS)
+    half_scores(1 - c)
     acc = jnp.zeros((COLS, 512), F32)
     for f in (0, 2, 1, 3):
         arrived(C.at[crows(3), fcols(f)], rx.at[2, f])
-        acc = acc + dots(3 * COLS, 4 * COLS, f * CH, (f + 1) * CH)
-    S[3 * COLS : 4 * COLS, :] = INV * acc
-    m_b, tot_b = partial_stats(3 * COLS, 4 * COLS)
+        acc = acc + dots(3 * COLS, 4 * COLS, slice(0, 512), f * CH, (f + 1) * CH)
+    S[3 * COLS : 4 * COLS, :] = acc
+    m_b, tot_b = partial_stats(3 * COLS, 4 * COLS, slice(0, 512))
+    m_a, tot_a = MT[0:1, :], MT[1:2, :]
 
     m = jnp.maximum(m_a, m_b)
     tot = tot_a * jnp.exp(m_a - m) + tot_b * jnp.exp(m_b - m)
@@ -206,11 +218,14 @@
             total = total + buf[i, 4:8, :] * jnp.exp(buf[i, 0:4, :] - top)
         return top, total
 
+    earlier = len(sent)
     for i in (*range(16, 24), *range(8, 16), *range(24, 32), *range(1, 8)):
         dy, dz, dc = i // 8, i // 2 % 4, i % 2
-        send(st1.at[0], st1.at[i], sst.at[i], rst1.at[i], dev(x, y + dy, z + dz, (c + dc) % 2))
-    for i in range(1, 32):
-        arrived(st1.at[i], rst1.at[i])
+        send(st1.at[0], st1.at[i], sst, rst1, dev(x, y + dy, z + dz, (c + dc) % 2))
+    del sent[earlier:]
+    flush()
+    others = st1.at[pl.ds(1, 31)]
+    arrived(others, rst1)
     top, total = merge(st1, 32)
     lt = top + jnp.log(total)
     log_total = jnp.concatenate([lt[j : j + 1, :] for j in range(4)], 1)
@@ -298,6 +313,7 @@
         for da in (2, 1, 3):
             src = T.at[rows_of(slot(0, 0, A + da)), fcols(f)]
             send(src, rA.at[da, :, fcols(f)], sA.at[da, f], rAs.at[da, f], at(A + da, B))
+    flush()
     for f in range(NF):
         cs = slice(f * CH, (f + 1) * CH)
         t = T[rows_of(A), cs].astype(F32)
@@ -312,8 +328,22 @@
         t = g0[:, cs] + rf1[:, cs].astype(F32) + rf2[:, cs].astype(F32)
         out[2 * ROWS :, cs] = t[0:NEG].astype(BF)
         out[ROWS : 2 * ROWS, cs] = t[NEG:COLS].astype(BF)
-    for cp in sent:
-        cp.wait_send()
+    flush()
+    pltpu.make_async_remote_copy(
+        src_ref=others, dst_ref=others, send_sem=sst, recv_sem=rst1, device_id=sib, device_id_type=MESH
+    ).wait_send()
+
+
+def placed(held, oq, op, on, sem):
+    copies = [
+        pltpu.make_async_copy(held.at[pl.ds(0, ROWS)], oq, sem.at[0]),
+        pltpu.make_async_copy(held.at[pl.ds(ROWS, ROWS)], op, sem.at[1]),
+        pltpu.make_async_copy(held.at[pl.ds(2 * ROWS, NEG)], on, sem.at[2]),
+    ]
+    for cp in copies:
+        cp.start()
+    for cp in copies:
+        cp.wait()
 
 
 def on_device(queries, document_vectors, negatives, positives, neg_ids):
@@ -353,14 +383,15 @@
             vm((COLS, D), BF),
             vm((COLS, D), BF),
             vm((32, 8, 128), F32),
+            vm((8, 512), F32),
             dma((5,)),
             dma((3, NF)),
             dma((3, NF)),
             dma((4, 4)),
             dma((16,)),
             dma((32,)),
-            dma((32,)),
-            dma((32,)),
+            dma,
+            dma,
             dma((3, NF)),
             dma((NF,)),
             dma((NF,)),
@@ -377,7 +408,13 @@
             collective_id=0, has_side_effects=True, vmem_limit_bytes=44 * 2**20
         ),
     )(*hbm)
-    return out[0:ROWS], out[ROWS : 2 * ROWS], out[2 * ROWS :]
+    parts = ((0, ROWS), (ROWS, ROWS), (2 * ROWS, NEG))
+    return pl.pallas_call(
+        placed,
+        out_shape=tuple(pltpu.HBM((n, D), BF) for _, n in parts),
+        in_specs=[pl.BlockSpec(memory_space=pltpu.VMEM)],
+        scratch_shapes=[dma((3,))],
+    )(pltpu.with_memory_space_constraint(out, pltpu.VMEM))
 
 
 def solution(mesh):

time: 64.4 us -> 63.5 us (0.986)
  local copies, waits for them, and re-layouts: 1.54 us -> 0 us
    slice x2 -> x0, local copies, waits for them, and re-layouts: 1.54 us -> none  [on_device(): return (out[0:ROWS], out[ROWS:2 * ROWS], out[2 * ROWS:])]
    pallas_call x0 -> x1, Pallas kernels: none -> 1.28 us  [on_device(): pl.pallas_call(placed, out_shape=tuple((pltpu.HBM((n, D), BF) for _, n in...]
    pallas_call x1, Pallas kernels: 61.8 us -> 61 us  [on_device(): pl.pallas_call(kernel, out_shape=pltpu.VMEM((2 * ROWS + NEG, D), BF), in_...]
where the time goes in v4:
time: 63.5 us; the launch traced here: 62.9 us
  Pallas kernels  62.3 us (98%)
  between operations  0.64 us (1%)
    pallas_call x1, Pallas kernels, on_device(): pl.pallas_call(kernel, out_shape=pltpu.VMEM((2 * ROWS + NEG, D), BF), in_...  61 us
    pallas_call x1, Pallas kernels, on_device(): pl.pallas_call(placed, out_shape=tuple((pltpu.HBM((n, D), BF) for _, n in...  1.28 us

profile of v4, /device:TPU:0, one launch (start us, length us, event | category | flops | bytes accessed | tf_op | source)
XLA Modules:
  0.0 62.9 jit_solution(4673132049807535237)
XLA Ops:
  0.6 61.0 %shard_map.76.held = bf16[96,4096]{1,0:T(8,128)(2,1)S(1)} custom-call(bf16[16,4096]{1,0:T(8,128)(2,1)} %q_in.1, bf16[16,4096]{1,0:T(8,128)(2,1)} %p_in.1, bf16[64,4096]{1,0:T(8,128)(2,1)} %n_in.1, s32[1,16]{1,0:T(1,128)} %bitcast.3, s32[7,16]{1,0:T(8,128)} %bitcast.2), custom_call_target="tpu_custom_call" | custom-call | tf_op jit(solution)/shard_map/pallas_call | solution.py:356
  61.7 1.3 %shard_map.77 = (bf16[16,4096]{1,0:T(8,128)(2,1)}, bf16[16,4096]{1,0:T(8,128)(2,1)}, bf16[64,4096]{1,0:T(8,128)(2,1)}) custom-call(bf16[96,4096]{1,0:T(8,128)(2,1)S(1)} %shard_map.76.held), custom_call_target="tpu_custom_call" | custom-call | tf_op jit(solution)/shard_map/pallas_call | solution.py:412

commit v5 on v4

--- a/solution.py
+++ b/solution.py
@@ -14,8 +14,12 @@
 NEG = 64
 ROWS = 16
 COLS = NEG + ROWS
-CH = 1024
+CH = 2048
 NF = D // CH
+CX = 1024
+NX = D // CX
+HX = NX // 2
+MIX = tuple(f for i in range(HX) for f in (i, i + HX))
 FLOOR = -1e30
 
 
@@ -68,6 +72,10 @@
             src_ref=dst, dst_ref=dst, send_sem=lsem.at[0], recv_sem=rs, device_id=sib, device_id_type=MESH
         ).wait_recv()
 
+    barrier = pltpu.get_barrier_semaphore()
+    greet = [right, left, at(A + 2, B), at(A, B + 2), at(A + 1, B), at(A - 1, B), at(A, B + 1), at(A, B - 1), sib]
+    for to in greet:
+        pl.semaphore_signal(barrier, inc=1, device_id=to, device_id_type=MESH)
     mine = slot(c, B, A)
     own_rows = rows_of(mine)
     local = [
@@ -79,10 +87,6 @@
     ]
     for cp in local:
         cp.start()
-    barrier = pltpu.get_barrier_semaphore()
-    greet = [at(A + 2, B), at(A, B + 2), at(A + 1, B), at(A - 1, B), at(A, B + 1), at(A, B - 1), right, left, sib]
-    for to in greet:
-        pl.semaphore_signal(barrier, inc=1, device_id=to, device_id_type=MESH)
     E[...] = jnp.zeros((128, 128), F32)
     for cp in local:
         cp.wait()
@@ -96,13 +100,16 @@
     def fcols(f):
         return pl.ds(f * CH, CH)
 
+    def xcols(f):
+        return pl.ds(f * CX, CX)
+
     def crows(k):
         return pl.ds(k * COLS, COLS)
 
-    for i in range(NF):
-        f, h = i, (i + 2) % 4
-        send(C.at[crows(0), fcols(f)], C.at[crows(1), fcols(f)], sx.at[0, f], rx.at[0, f], right)
-        send(C.at[crows(0), fcols(h)], C.at[crows(2), fcols(h)], sx.at[1, h], rx.at[1, h], left)
+    for f in range(NX):
+        h = (f + HX) % NX
+        send(C.at[crows(0), xcols(f)], C.at[crows(1), xcols(f)], sx.at[0, f], rx.at[0, f], right)
+        send(C.at[crows(0), xcols(h)], C.at[crows(2), xcols(h)], sx.at[1, h], rx.at[1, h], left)
     for da in (1, 3, 2):
         send(Q.at[own_rows], Q.at[own_rows], sq.at[0, da], rq.at[mine], at(A + da, B))
 
@@ -130,11 +137,11 @@
             to_sib(r, 4 + 4 * i + da)
 
     def columns_on(f):
-        arrived(C.at[crows(1), fcols(f)], rx.at[0, f])
-        send(C.at[crows(1), fcols(f)], C.at[crows(3), fcols(f)], sx.at[2, f], rx.at[2, f], right)
-        h = f + 2
-        arrived(C.at[crows(2), fcols(h)], rx.at[1, h])
-        send(C.at[crows(2), fcols(h)], C.at[crows(3), fcols(h)], sx.at[2, h], rx.at[2, h], left)
+        arrived(C.at[crows(1), xcols(f)], rx.at[0, f])
+        send(C.at[crows(1), xcols(f)], C.at[crows(3), xcols(f)], sx.at[2, f], rx.at[2, f], right)
+        h = f + HX
+        arrived(C.at[crows(2), xcols(h)], rx.at[1, h])
+        send(C.at[crows(2), xcols(h)], C.at[crows(3), xcols(h)], sx.at[2, h], rx.at[2, h], left)
 
     for da in (0, 1, 3):
         spread(da)
@@ -187,18 +194,18 @@
         MT[0:1, qs] = m
         MT[1:2, qs] = tot
 
-    for f in (2, 3):
-        arrived(C.at[crows(1), fcols(f)], rx.at[0, f])
-        arrived(C.at[crows(2), fcols(f - 2)], rx.at[1, f - 2])
+    for f in range(HX):
+        arrived(C.at[crows(1), xcols(f + HX)], rx.at[0, f + HX])
+        arrived(C.at[crows(2), xcols(f)], rx.at[1, f])
     half_scores(c)
     for k in range(16):
         r = (1 - c) * 16 + k
         arrived(Q.at[rows_of(r)], rq.at[r])
     half_scores(1 - c)
     acc = jnp.zeros((COLS, 512), F32)
-    for f in (0, 2, 1, 3):
-        arrived(C.at[crows(3), fcols(f)], rx.at[2, f])
-        acc = acc + dots(3 * COLS, 4 * COLS, slice(0, 512), f * CH, (f + 1) * CH)
+    for f in MIX:
+        arrived(C.at[crows(3), xcols(f)], rx.at[2, f])
+        acc = acc + dots(3 * COLS, 4 * COLS, slice(0, 512), f * CX, (f + 1) * CX)
     S[3 * COLS : 4 * COLS, :] = acc
     m_b, tot_b = partial_stats(3 * COLS, 4 * COLS, slice(0, 512))
     m_a, tot_a = MT[0:1, :], MT[1:2, :]
@@ -237,13 +244,13 @@
         W[r1:r2, :] = (jnp.exp(S[r1:r2, :] - log_total) - MU[r1:r2, :]).astype(BF)
 
     def col_grad(lo, hi, f):
-        return INV * jnp.dot(W[lo:hi, :], Q[:, f * CH : (f + 1) * CH], preferred_element_type=F32)
+        return INV * jnp.dot(W[lo:hi, :], Q[:, f * CX : (f + 1) * CX], preferred_element_type=F32)
 
     weights(3)
-    for f in (0, 2, 1, 3):
-        g3[:, f * CH : (f + 1) * CH] = col_grad(3 * COLS, 4 * COLS, f).astype(BF)
-        to = right if f < 2 else left
-        send(g3.at[:, fcols(f)], rx2.at[:, fcols(f)], sg.at[0, f], rg2.at[f], to)
+    for f in MIX:
+        g3[:, f * CX : (f + 1) * CX] = col_grad(3 * COLS, 4 * COLS, f).astype(BF)
+        to = right if f < HX else left
+        send(g3.at[:, xcols(f)], rx2.at[:, xcols(f)], sg.at[0, f], rg2.at[f], to)
     for k in (0, 1, 2):
         weights(k)
 
@@ -259,18 +266,18 @@
     def group(b, i):
         return rows_of(slot(0, b, 2 * i), 32)
 
+    for f in MIX:
+        cs = slice(f * CX, (f + 1) * CX)
+        g12[:, cs] = col_grad(COLS, 3 * COLS, f)
+        if f < HX:
+            gsend[0:COLS, cs] = g12[0:COLS, cs].astype(BF)
+            send(gsend.at[pl.ds(0, COLS), xcols(f)], rf2.at[:, xcols(f)], sg.at[1, f], rgf2.at[f], left)
+        else:
+            gsend[COLS:, cs] = g12[COLS:, cs].astype(BF)
+            send(gsend.at[pl.ds(COLS, COLS), xcols(f)], rf1.at[:, xcols(f)], sg.at[1, f], rgf1.at[f], right)
     for f in range(NF):
         sibs[:, f * CH : (f + 1) * CH] = query_grad(1 - c, f).astype(BF)
         send(sibs.at[:, fcols(f)], rsib.at[:, fcols(f)], ssib.at[f], rsibs.at[f], sib)
-    for f in range(NF):
-        cs = slice(f * CH, (f + 1) * CH)
-        g12[:, cs] = col_grad(COLS, 3 * COLS, f)
-        if f < 2:
-            gsend[0:COLS, cs] = g12[0:COLS, cs].astype(BF)
-            send(gsend.at[pl.ds(0, COLS), fcols(f)], rf2.at[:, fcols(f)], sg.at[1, f], rgf2.at[f], left)
-        else:
-            gsend[COLS:, cs] = g12[COLS:, cs].astype(BF)
-            send(gsend.at[pl.ds(COLS, COLS), fcols(f)], rf1.at[:, fcols(f)], sg.at[1, f], rgf1.at[f], right)
     for f in range(NF):
         ownq[:, f * CH : (f + 1) * CH] = query_grad(c, f)
     for f in range(NF):
@@ -291,17 +298,17 @@
             t = G[group(B + db, i), cs].astype(F32) + rB2[h, cs].astype(F32)
             gB[h, cs] = t.astype(BF)
             send(gB.at[h, fcols(f)], rB.at[i, h, fcols(f)], sB.at[2, i, f], rBs.at[i, i, f], at(A, B + db))
-    for f in (0, 2, 1, 3):
-        cs = slice(f * CH, (f + 1) * CH)
-        arrived(rx2.at[:, fcols(f)], rg2.at[f])
-        if f < 2:
+    for f in MIX:
+        cs = slice(f * CX, (f + 1) * CX)
+        arrived(rx2.at[:, xcols(f)], rg2.at[f])
+        if f < HX:
             gsend[COLS:, cs] = (g12[COLS:, cs] + rx2[:, cs].astype(F32)).astype(BF)
-            send(gsend.at[pl.ds(COLS, COLS), fcols(f)], rf1.at[:, fcols(f)], sg.at[2, f], rgf1.at[f], right)
+            send(gsend.at[pl.ds(COLS, COLS), xcols(f)], rf1.at[:, xcols(f)], sg.at[2, f], rgf1.at[f], right)
         else:
             gsend[0:COLS, cs] = (g12[0:COLS, cs] + rx2[:, cs].astype(F32)).astype(BF)
-            send(gsend.at[pl.ds(0, COLS), fcols(f)], rf2.at[:, fcols(f)], sg.at[2, f], rgf2.at[f], left)
-    for f in range(NF):
-        g0[:, f * CH : (f + 1) * CH] = col_grad(0, COLS, f)
+            send(gsend.at[pl.ds(0, COLS), xcols(f)], rf2.at[:, xcols(f)], sg.at[2, f], rgf2.at[f], left)
+    for f in range(NX):
+        g0[:, f * CX : (f + 1) * CX] = col_grad(0, COLS, f)
     for f in range(NF):
         cs = slice(f * CH, (f + 1) * CH)
         t = G[rows_of(slot(0, B, 0), 64), cs].astype(F32)
@@ -321,10 +328,10 @@
             arrived(rA.at[da, :, fcols(f)], rAs.at[da, f])
             t = t + rA[da, :, cs].astype(F32)
         out[0:ROWS, cs] = t.astype(BF)
-    for f in (2, 0, 3, 1):
-        cs = slice(f * CH, (f + 1) * CH)
-        arrived(rf1.at[:, fcols(f)], rgf1.at[f])
-        arrived(rf2.at[:, fcols(f)], rgf2.at[f])
+    for f in MIX:
+        cs = slice(f * CX, (f + 1) * CX)
+        arrived(rf1.at[:, xcols(f)], rgf1.at[f])
+        arrived(rf2.at[:, xcols(f)], rgf2.at[f])
         t = g0[:, cs] + rf1[:, cs].astype(F32) + rf2[:, cs].astype(F32)
         out[2 * ROWS :, cs] = t[0:NEG].astype(BF)
         out[ROWS : 2 * ROWS, cs] = t[NEG:COLS].astype(BF)
@@ -385,17 +392,17 @@
             vm((32, 8, 128), F32),
             vm((8, 512), F32),
             dma((5,)),
-            dma((3, NF)),
-            dma((3, NF)),
+            dma((3, NX)),
+            dma((3, NX)),
             dma((4, 4)),
             dma((16,)),
             dma((32,)),
             dma,
             dma,
-            dma((3, NF)),
-            dma((NF,)),
-            dma((NF,)),
-            dma((NF,)),
+            dma((3, NX)),
+            dma((NX,)),
+            dma((NX,)),
+            dma((NX,)),
             dma((NF,)),
             dma((NF,)),
             dma((3, 2, NF)),

time: 63.5 us -> 63 us (level)
  no operation moved by 1% of the time
where the time goes in v5:
time: 63 us; the launch traced here: 62.5 us
  Pallas kernels  61.9 us (98%)
  between operations  0.64 us (1%)
    pallas_call x1, Pallas kernels, on_device(): pl.pallas_call(kernel, out_shape=pltpu.VMEM((2 * ROWS + NEG, D), BF), in_...  60.6 us
    pallas_call x1, Pallas kernels, on_device(): pl.pallas_call(placed, out_shape=tuple((pltpu.HBM((n, D), BF) for _, n in...  1.28 us

profile of v5, /device:TPU:0, one launch (start us, length us, event | category | flops | bytes accessed | tf_op | source)
XLA Modules:
  0.0 62.5 jit_solution(2965687481681922572)
XLA Ops:
  0.6 60.6 %shard_map.76.held = bf16[96,4096]{1,0:T(8,128)(2,1)S(1)} custom-call(bf16[16,4096]{1,0:T(8,128)(2,1)} %q_in.1, bf16[16,4096]{1,0:T(8,128)(2,1)} %p_in.1, bf16[64,4096]{1,0:T(8,128)(2,1)} %n_in.1, s32[1,16]{1,0:T(1,128)} %bitcast.3, s32[7,16]{1,0:T(8,128)} %bitcast.2), custom_call_target="tpu_custom_call" | custom-call | tf_op jit(solution)/shard_map/pallas_call | solution.py:363
  61.2 1.3 %shard_map.77 = (bf16[16,4096]{1,0:T(8,128)(2,1)}, bf16[16,4096]{1,0:T(8,128)(2,1)}, bf16[64,4096]{1,0:T(8,128)(2,1)}) custom-call(bf16[96,4096]{1,0:T(8,128)(2,1)S(1)} %shard_map.76.held), custom_call_target="tpu_custom_call" | custom-call | tf_op jit(solution)/shard_map/pallas_call | solution.py:419

commit v6 on v5

--- a/solution.py
+++ b/solution.py
@@ -20,6 +20,7 @@
 NX = D // CX
 HX = NX // 2
 MIX = tuple(f for i in range(HX) for f in (i, i + HX))
+GATHER = ((0, 1536), (1536, 512), (2048, 1536), (3584, 512))
 FLOOR = -1e30
 
 
@@ -87,29 +88,34 @@
     ]
     for cp in local:
         cp.start()
+    local[0].wait()
+    local[1].wait()
+    pl.semaphore_wait(barrier, len(greet))
+
+    def fcols(f):
+        return pl.ds(f * CH, CH)
+
+    def xcols(f):
+        return pl.ds(f * CX, CX)
+
+    def gcols(f):
+        return pl.ds(*GATHER[f])
+
+    def crows(k):
+        return pl.ds(k * COLS, COLS)
+
+    for f in range(NX):
+        h = (f + HX) % NX
+        send(C.at[crows(0), gcols(f)], C.at[crows(1), gcols(f)], sx.at[0, f], rx.at[0, f], right)
+        send(C.at[crows(0), gcols(h)], C.at[crows(2), gcols(h)], sx.at[1, h], rx.at[1, h], left)
     E[...] = jnp.zeros((128, 128), F32)
-    for cp in local:
+    for cp in local[2:]:
         cp.wait()
     for r, part in ((0, ID[...]), (7, PO[...])):
         n = part.shape[0]
         E[r : r + n, 0:ROWS] = (part // 128).astype(F32)
         E[8 + r : 8 + r + n, 0:ROWS] = (part % 128).astype(F32)
     Q[own_rows, D : D + EXT] = jnp.transpose(E[...])[0:ROWS].astype(BF)
-    pl.semaphore_wait(barrier, len(greet))
-
-    def fcols(f):
-        return pl.ds(f * CH, CH)
-
-    def xcols(f):
-        return pl.ds(f * CX, CX)
-
-    def crows(k):
-        return pl.ds(k * COLS, COLS)
-
-    for f in range(NX):
-        h = (f + HX) % NX
-        send(C.at[crows(0), xcols(f)], C.at[crows(1), xcols(f)], sx.at[0, f], rx.at[0, f], right)
-        send(C.at[crows(0), xcols(h)], C.at[crows(2), xcols(h)], sx.at[1, h], rx.at[1, h], left)
     for da in (1, 3, 2):
         send(Q.at[own_rows], Q.at[own_rows], sq.at[0, da], rq.at[mine], at(A + da, B))
 
@@ -137,11 +143,11 @@
             to_sib(r, 4 + 4 * i + da)
 
     def columns_on(f):
-        arrived(C.at[crows(1), xcols(f)], rx.at[0, f])
-        send(C.at[crows(1), xcols(f)], C.at[crows(3), xcols(f)], sx.at[2, f], rx.at[2, f], right)
+        arrived(C.at[crows(1), gcols(f)], rx.at[0, f])
+        send(C.at[crows(1), gcols(f)], C.at[crows(3), gcols(f)], sx.at[2, f], rx.at[2, f], right)
         h = f + HX
-        arrived(C.at[crows(2), xcols(h)], rx.at[1, h])
-        send(C.at[crows(2), xcols(h)], C.at[crows(3), xcols(h)], sx.at[2, h], rx.at[2, h], left)
+        arrived(C.at[crows(2), gcols(h)], rx.at[1, h])
+        send(C.at[crows(2), gcols(h)], C.at[crows(3), gcols(h)], sx.at[2, h], rx.at[2, h], left)
 
     for da in (0, 1, 3):
         spread(da)
@@ -195,8 +201,8 @@
         MT[1:2, qs] = tot
 
     for f in range(HX):
-        arrived(C.at[crows(1), xcols(f + HX)], rx.at[0, f + HX])
-        arrived(C.at[crows(2), xcols(f)], rx.at[1, f])
+        arrived(C.at[crows(1), gcols(f + HX)], rx.at[0, f + HX])
+        arrived(C.at[crows(2), gcols(f)], rx.at[1, f])
     half_scores(c)
     for k in range(16):
         r = (1 - c) * 16 + k
@@ -204,8 +210,8 @@
     half_scores(1 - c)
     acc = jnp.zeros((COLS, 512), F32)
     for f in MIX:
-        arrived(C.at[crows(3), xcols(f)], rx.at[2, f])
-        acc = acc + dots(3 * COLS, 4 * COLS, slice(0, 512), f * CX, (f + 1) * CX)
+        arrived(C.at[crows(3), gcols(f)], rx.at[2, f])
+        acc = acc + dots(3 * COLS, 4 * COLS, slice(0, 512), GATHER[f][0], sum(GATHER[f]))
     S[3 * COLS : 4 * COLS, :] = acc
     m_b, tot_b = partial_stats(3 * COLS, 4 * COLS, slice(0, 512))
     m_a, tot_a = MT[0:1, :], MT[1:2, :]

time: 63 us -> 62.9 us (level)
  no operation moved by 1% of the time
where the time goes in v6:
time: 62.9 us; the launch traced here: 62.4 us
  Pallas kernels  61.8 us (98%)
  between operations  0.64 us (1%)
    pallas_call x1, Pallas kernels, on_device(): pl.pallas_call(kernel, out_shape=pltpu.VMEM((2 * ROWS + NEG, D), BF), in_...  60.5 us
    pallas_call x1, Pallas kernels, on_device(): pl.pallas_call(placed, out_shape=tuple((pltpu.HBM((n, D), BF) for _, n in...  1.28 us

profile of v6, /device:TPU:0, one launch (start us, length us, event | category | flops | bytes accessed | tf_op | source)
XLA Modules:
  0.0 62.4 jit_solution(6282859845542055628)
XLA Ops:
  0.6 60.5 %shard_map.76.held = bf16[96,4096]{1,0:T(8,128)(2,1)S(1)} custom-call(bf16[16,4096]{1,0:T(8,128)(2,1)} %q_in.1, bf16[16,4096]{1,0:T(8,128)(2,1)} %p_in.1, bf16[64,4096]{1,0:T(8,128)(2,1)} %n_in.1, s32[1,16]{1,0:T(1,128)} %bitcast.3, s32[7,16]{1,0:T(8,128)} %bitcast.2), custom_call_target="tpu_custom_call" | custom-call | tf_op jit(solution)/shard_map/pallas_call | solution.py:369
  61.1 1.3 %shard_map.77 = (bf16[16,4096]{1,0:T(8,128)(2,1)}, bf16[16,4096]{1,0:T(8,128)(2,1)}, bf16[64,4096]{1,0:T(8,128)(2,1)}) custom-call(bf16[96,4096]{1,0:T(8,128)(2,1)S(1)} %shard_map.76.held), custom_call_target="tpu_custom_call" | custom-call | tf_op jit(solution)/shard_map/pallas_call | solution.py:425

commit v7 on v6

--- a/solution.py
+++ b/solution.py
@@ -22,6 +22,7 @@
 MIX = tuple(f for i in range(HX) for f in (i, i + HX))
 GATHER = ((0, 1536), (1536, 512), (2048, 1536), (3584, 512))
 FLOOR = -1e30
+RETURN = ((0, 512), (512, 1536), (2048, 512), (2560, 1536))
 
 
 def kernel(
@@ -95,11 +96,11 @@
     def fcols(f):
         return pl.ds(f * CH, CH)
 
-    def xcols(f):
-        return pl.ds(f * CX, CX)
-
     def gcols(f):
         return pl.ds(*GATHER[f])
+
+    def scols(f):
+        return pl.ds(*RETURN[f])
 
     def crows(k):
         return pl.ds(k * COLS, COLS)
@@ -250,13 +251,13 @@
         W[r1:r2, :] = (jnp.exp(S[r1:r2, :] - log_total) - MU[r1:r2, :]).astype(BF)
 
     def col_grad(lo, hi, f):
-        return INV * jnp.dot(W[lo:hi, :], Q[:, f * CX : (f + 1) * CX], preferred_element_type=F32)
+        return INV * jnp.dot(W[lo:hi, :], Q[:, RETURN[f][0] : sum(RETURN[f])], preferred_element_type=F32)
 
     weights(3)
     for f in MIX:
-        g3[:, f * CX : (f + 1) * CX] = col_grad(3 * COLS, 4 * COLS, f).astype(BF)
+        g3[:, RETURN[f][0] : sum(RETURN[f])] = col_grad(3 * COLS, 4 * COLS, f).astype(BF)
         to = right if f < HX else left
-        send(g3.at[:, xcols(f)], rx2.at[:, xcols(f)], sg.at[0, f], rg2.at[f], to)
+        send(g3.at[:, scols(f)], rx2.at[:, scols(f)], sg.at[0, f], rg2.at[f], to)
     for k in (0, 1, 2):
         weights(k)
 
@@ -273,14 +274,14 @@
         return rows_of(slot(0, b, 2 * i), 32)
 
     for f in MIX:
-        cs = slice(f * CX, (f + 1) * CX)
+        cs = slice(RETURN[f][0], sum(RETURN[f]))
         g12[:, cs] = col_grad(COLS, 3 * COLS, f)
         if f < HX:
             gsend[0:COLS, cs] = g12[0:COLS, cs].astype(BF)
-            send(gsend.at[pl.ds(0, COLS), xcols(f)], rf2.at[:, xcols(f)], sg.at[1, f], rgf2.at[f], left)
+            send(gsend.at[pl.ds(0, COLS), scols(f)], rf2.at[:, scols(f)], sg.at[1, f], rgf2.at[f], left)
         else:
             gsend[COLS:, cs] = g12[COLS:, cs].astype(BF)
-            send(gsend.at[pl.ds(COLS, COLS), xcols(f)], rf1.at[:, xcols(f)], sg.at[1, f], rgf1.at[f], right)
+            send(gsend.at[pl.ds(COLS, COLS), scols(f)], rf1.at[:, scols(f)], sg.at[1, f], rgf1.at[f], right)
     for f in range(NF):
         sibs[:, f * CH : (f + 1) * CH] = query_grad(1 - c, f).astype(BF)
         send(sibs.at[:, fcols(f)], rsib.at[:, fcols(f)], ssib.at[f], rsibs.at[f], sib)
@@ -305,16 +306,16 @@
             gB[h, cs] = t.astype(BF)
             send(gB.at[h, fcols(f)], rB.at[i, h, fcols(f)], sB.at[2, i, f], rBs.at[i, i, f], at(A, B + db))
     for f in MIX:
-        cs = slice(f * CX, (f + 1) * CX)
-        arrived(rx2.at[:, xcols(f)], rg2.at[f])
+        cs = slice(RETURN[f][0], sum(RETURN[f]))
+        arrived(rx2.at[:, scols(f)], rg2.at[f])
         if f < HX:
             gsend[COLS:, cs] = (g12[COLS:, cs] + rx2[:, cs].astype(F32)).astype(BF)
-            send(gsend.at[pl.ds(COLS, COLS), xcols(f)], rf1.at[:, xcols(f)], sg.at[2, f], rgf1.at[f], right)
+            send(gsend.at[pl.ds(COLS, COLS), scols(f)], rf1.at[:, scols(f)], sg.at[2, f], rgf1.at[f], right)
         else:
             gsend[0:COLS, cs] = (g12[0:COLS, cs] + rx2[:, cs].astype(F32)).astype(BF)
-            send(gsend.at[pl.ds(0, COLS), xcols(f)], rf2.at[:, xcols(f)], sg.at[2, f], rgf2.at[f], left)
+            send(gsend.at[pl.ds(0, COLS), scols(f)], rf2.at[:, scols(f)], sg.at[2, f], rgf2.at[f], left)
     for f in range(NX):
-        g0[:, f * CX : (f + 1) * CX] = col_grad(0, COLS, f)
+        g0[:, RETURN[f][0] : sum(RETURN[f])] = col_grad(0, COLS, f)
     for f in range(NF):
         cs = slice(f * CH, (f + 1) * CH)
         t = G[rows_of(slot(0, B, 0), 64), cs].astype(F32)
@@ -335,9 +336,9 @@
             t = t + rA[da, :, cs].astype(F32)
         out[0:ROWS, cs] = t.astype(BF)
     for f in MIX:
-        cs = slice(f * CX, (f + 1) * CX)
-        arrived(rf1.at[:, xcols(f)], rgf1.at[f])
-        arrived(rf2.at[:, xcols(f)], rgf2.at[f])
+        cs = slice(RETURN[f][0], sum(RETURN[f]))
+        arrived(rf1.at[:, scols(f)], rgf1.at[f])
+        arrived(rf2.at[:, scols(f)], rgf2.at[f])
         t = g0[:, cs] + rf1[:, cs].astype(F32) + rf2[:, cs].astype(F32)
         out[2 * ROWS :, cs] = t[0:NEG].astype(BF)
         out[ROWS : 2 * ROWS, cs] = t[NEG:COLS].astype(BF)

time: 62.9 us -> 62.9 us (level)
  no operation moved by 1% of the time
where the time goes in v7:
time: 62.9 us; the launch traced here: 62.4 us
  Pallas kernels  61.7 us (98%)
  between operations  0.64 us (1%)
    pallas_call x1, Pallas kernels, on_device(): pl.pallas_call(kernel, out_shape=pltpu.VMEM((2 * ROWS + NEG, D), BF), in_...  60.4 us
    pallas_call x1, Pallas kernels, on_device(): pl.pallas_call(placed, out_shape=tuple((pltpu.HBM((n, D), BF) for _, n in...  1.28 us

profile of v7, /device:TPU:0, one launch (start us, length us, event | category | flops | bytes accessed | tf_op | source)
XLA Modules:
  0.0 62.4 jit_solution(18043381306273568614)
XLA Ops:
  0.6 60.4 %shard_map.76.held = bf16[96,4096]{1,0:T(8,128)(2,1)S(1)} custom-call(bf16[16,4096]{1,0:T(8,128)(2,1)} %q_in.1, bf16[16,4096]{1,0:T(8,128)(2,1)} %p_in.1, bf16[64,4096]{1,0:T(8,128)(2,1)} %n_in.1, s32[1,16]{1,0:T(1,128)} %bitcast.3, s32[7,16]{1,0:T(8,128)} %bitcast.2), custom_call_target="tpu_custom_call" | custom-call | tf_op jit(solution)/shard_map/pallas_call | solution.py:370
  61.1 1.3 %shard_map.77 = (bf16[16,4096]{1,0:T(8,128)(2,1)}, bf16[16,4096]{1,0:T(8,128)(2,1)}, bf16[64,4096]{1,0:T(8,128)(2,1)}) custom-call(bf16[96,4096]{1,0:T(8,128)(2,1)S(1)} %shard_map.76.held), custom_call_target="tpu_custom_call" | custom-call | tf_op jit(solution)/shard_map/pallas_call | solution.py:426

commit v8 on v7

--- a/solution.py
+++ b/solution.py
@@ -233,11 +233,16 @@
         return top, total
 
     earlier = len(sent)
-    for i in (*range(16, 24), *range(8, 16), *range(24, 32), *range(1, 8)):
+    def hops(i):
+        dy, dz = i // 8, i // 2 % 4
+        return min(dy, 4 - dy) + min(dz, 4 - dz)
+
+    for i in sorted(range(1, 32), key=hops, reverse=True):
         dy, dz, dc = i // 8, i // 2 % 4, i % 2
         send(st1.at[0], st1.at[i], sst, rst1, dev(x, y + dy, z + dz, (c + dc) % 2))
     del sent[earlier:]
     flush()
+    S[3 * COLS : 4 * COLS, :] = jnp.exp(S[3 * COLS : 4 * COLS, :] - m)
     others = st1.at[pl.ds(1, 31)]
     arrived(others, rst1)
     top, total = merge(st1, 32)
@@ -253,7 +258,10 @@
     def col_grad(lo, hi, f):
         return INV * jnp.dot(W[lo:hi, :], Q[:, RETURN[f][0] : sum(RETURN[f])], preferred_element_type=F32)
 
-    weights(3)
+    scale = jnp.exp(m - log_total)
+    r0, r1, r2 = 3 * COLS, 3 * COLS + NEG, 4 * COLS
+    W[r0:r1, :] = ((S[r0:r1, :] * scale).astype(BF).astype(F32) * MU[r0:r1, :]).astype(BF)
+    W[r1:r2, :] = (S[r1:r2, :] * scale - MU[r1:r2, :]).astype(BF)
     for f in MIX:
         g3[:, RETURN[f][0] : sum(RETURN[f])] = col_grad(3 * COLS, 4 * COLS, f).astype(BF)
         to = right if f < HX else left

time: 62.9 us -> 63.1 us (level)
  no operation moved by 1% of the time
where the time goes in v8:
time: 63.1 us; the launch traced here: 62.5 us
  Pallas kernels  61.8 us (98%)
  between operations  0.64 us (1%)
    pallas_call x1, Pallas kernels, on_device(): pl.pallas_call(kernel, out_shape=pltpu.VMEM((2 * ROWS + NEG, D), BF), in_...  60.5 us
    pallas_call x1, Pallas kernels, on_device(): pl.pallas_call(placed, out_shape=tuple((pltpu.HBM((n, D), BF) for _, n in...  1.28 us

profile of v8, /device:TPU:0, one launch (start us, length us, event | category | flops | bytes accessed | tf_op | source)
XLA Modules:
  0.0 62.5 jit_solution(5622463394377702121)
XLA Ops:
  0.6 60.5 %shard_map.76.held = bf16[96,4096]{1,0:T(8,128)(2,1)S(1)} custom-call(bf16[16,4096]{1,0:T(8,128)(2,1)} %q_in.1, bf16[16,4096]{1,0:T(8,128)(2,1)} %p_in.1, bf16[64,4096]{1,0:T(8,128)(2,1)} %n_in.1, s32[1,16]{1,0:T(1,128)} %bitcast.3, s32[7,16]{1,0:T(8,128)} %bitcast.2), custom_call_target="tpu_custom_call" | custom-call | tf_op jit(solution)/shard_map/pallas_call | solution.py:378
  61.2 1.3 %shard_map.77 = (bf16[16,4096]{1,0:T(8,128)(2,1)}, bf16[16,4096]{1,0:T(8,128)(2,1)}, bf16[64,4096]{1,0:T(8,128)(2,1)}) custom-call(bf16[96,4096]{1,0:T(8,128)(2,1)S(1)} %shard_map.76.held), custom_call_target="tpu_custom_call" | custom-call | tf_op jit(solution)/shard_map/pallas_call | solution.py:434
